TPU v7x, 128 devices: a whole 4x4x4 slice. The times are simulated.
128 devices in a mesh: row: 8 (over z, core), col: 16 (over y, x).
Axes of the slice: x: 4, y: 4, z: 4, core: 2. Of those that a mesh axis runs over, the one named last changes fastest.
Arguments:
- trailing: float32 [20480, 20480], P('row', 'col'), may hold values from -24 to 24
- panel_block: float32 [20480, 128], P(('row', 'col')), may hold values from -0.2795085 to 0.2795085
Outputs:
- trailing_out: float32 [20480, 20480], P('row', 'col')
- r_factor: float32 [128, 128], replicated
- first_factor: float32 [128, 128], replicated
All inputs are finite; a program needn't handle non-finite values.
Results may differ from a plain program's by a relative error of at most 0.0003.
Values sent between devices are 32-bit elements; how exact they have to be, the bound alone decides.
A program may use at most 128 MiB of HBM per device.

v0:
```python
import jax
import jax.numpy as jnp
from jax import lax
from jax.sharding import PartitionSpec as P

HIGHEST = lax.Precision.HIGHEST


def matmul(first, second):
    return jnp.dot(first, second, preferred_element_type=jnp.float32, precision=HIGHEST)


def column_block(block_rows, col_width, my_column):
    gathered = lax.all_gather(block_rows, "row", axis=0, tiled=True)
    return lax.dynamic_slice_in_dim(gathered, my_column * col_width, col_width, 0)


def on_device(trailing, panel_block):
    col_width = trailing.shape[1]
    my_column = lax.axis_index("col")
    gram_one = lax.psum(matmul(panel_block.T, panel_block), ("row", "col"))
    low_one = jnp.linalg.cholesky(gram_one)
    first_q = lax.linalg.triangular_solve(
        low_one, panel_block, left_side=False, lower=True, transpose_a=True
    )
    gram_two = lax.psum(matmul(first_q.T, first_q), ("row", "col"))
    low_two = jnp.linalg.cholesky(gram_two)
    ortho_basis = lax.linalg.triangular_solve(
        low_two, first_q, left_side=False, lower=True, transpose_a=True
    )
    r_factor = matmul(low_two.T, low_one.T)
    basis_block = lax.all_gather(ortho_basis, "col", axis=0, tiled=True)
    basis_cols = column_block(basis_block, col_width, my_column)
    products = lax.psum_scatter(
        matmul(trailing, basis_cols), "col", scatter_dimension=0, tiled=True
    )
    projected = lax.psum(matmul(ortho_basis.T, products), ("row", "col"))
    correction = 2.0 * (products - matmul(ortho_basis, projected))
    correction_rows = lax.all_gather(correction, "col", axis=0, tiled=True)
    correction_cols = column_block(correction_rows, col_width, my_column)
    left_factor = jnp.concatenate([basis_block, correction_rows], axis=1)
    right_factor = jnp.concatenate([correction_cols, basis_cols], axis=1)
    trailing_out = trailing - matmul(left_factor, right_factor.T)
    return (trailing_out, r_factor, low_one.T)


def solution(mesh):
    in_specs = (P("row", "col"), P(("row", "col"), None))
    out_specs = (P("row", "col"), P(), P())
    return jax.shard_map(
        on_device, mesh=mesh, in_specs=in_specs, out_specs=out_specs, check_vma=False
    )
```

profile of v0, /device:TPU:1, one launch (start us, length us, event | category | flops | bytes accessed | tf_op | source)
XLA Modules:
  0.0 798.4 jit_solution(5109152109191603435)
XLA Ops:
  7.2 0.0 all-reduce.4.cloned.1.call-start
  7.2 0.8 copy-done
  8.1 1.1 fusion.28
  9.1 0.0 all-reduce.4.cloned.1.call-update
  9.2 0.0 all-reduce.6.cloned.1.call-start
  9.2 145.2 %all-reduce.4.cloned.1.call-done = f32[128,128]{0,1:T(8,128)} async-done(((f32[128,128]{0,1:T(8,128)}), f32[128,128]{0,1:T(8,128)}) %all-reduce.4.cloned.1.call-update) | async-done | bytes 65552 | tf_op jit(solution)/shard_map/psum | solution.py:21
  154.4 0.9 copy.6
  155.3 0.9 fusion.10
  156.2 11.7 %cholesky.44 = f32[128,128]{1,0:T(8,128)S(1)} custom-call(f32[128,128]{1,0:T(8,128)S(1)} %fusion.10), custom_call_target="Cholesky" | custom-call | tf_op jit(solution)/shard_map/jit(cholesky)/cholesky | solution.py:22
  167.9 0.7 compare_reduce_fusion.1
  168.6 0.6 fusion.19
  169.3 9.8 %custom-call.6 = f32[1,128,128]{1,2,0:T(8,128)S(1)} custom-call(f32[1,128,128]{2,1,0:T(8,128)S(1)} %get-tuple-element.9), custom_call_target="InvertDiagBlocksLowerTriangular" | custom-call | tf_op jit(solution)/shard_map/triangular_solve/custom-call.0 | solution.py:23
  179.1 0.2 convolution_bitcast_fusion.2
  179.3 1.1 fusion.29
  180.4 0.0 all-reduce.6.cloned.1.call-update
  180.4 0.2 all-gather.5.cloned.1.call-start
  180.6 134.6 %all-reduce.6.cloned.1.call-done = f32[128,128]{0,1:T(8,128)} async-done(((f32[128,128]{0,1:T(8,128)}), f32[128,128]{0,1:T(8,128)}) %all-reduce.6.cloned.1.call-update) | async-done | bytes 65552 | tf_op jit(solution)/shard_map/psum | solution.py:26
  315.3 0.9 copy.8
  316.2 0.9 fusion.8
  317.1 11.7 %cholesky.55 = f32[128,128]{1,0:T(8,128)S(1)} custom-call(f32[128,128]{1,0:T(8,128)S(1)} %fusion.8), custom_call_target="Cholesky" | custom-call | tf_op jit(solution)/shard_map/jit(cholesky)/cholesky | solution.py:27
  328.8 0.7 compare_reduce_fusion
  329.5 0.7 select_bitcast_fusion
  330.2 9.8 %custom-call.7 = f32[1,128,128]{1,2,0:T(8,128)S(1)} custom-call(f32[1,128,128]{2,1,0:T(8,128)S(1)} %select_bitcast_fusion), custom_call_target="InvertDiagBlocksLowerTriangular" | custom-call | tf_op jit(solution)/shard_map/triangular_solve/custom-call.0 | solution.py:28
  340.0 0.9 convolution_bitcast_fusion.1
  340.9 0.0 all-gather.5.cloned.1.call-update
  340.9 0.0 all-gather.7.cloned.1.call-start
  341.0 39.4 %all-gather.5.cloned.1.call-done = f32[2560,128]{1,0:T(8,128)} async-done(((f32[160,128]{1,0:T(8,128)}), f32[2560,128]{1,0:T(8,128)}) %all-gather.5.cloned.1.call-update) | async-done | bytes 1310736 | tf_op jit(solution)/shard_map/all_gather | solution.py:32
  380.3 0.0 all-gather.7.cloned.1.call-update
  380.3 0.0 reduce-scatter.2.cloned.1.call-start
  380.4 60.9 %all-gather.7.cloned.1.call-done = f32[20480,128]{1,0:T(8,128)} async-done(((f32[2560,128]{1,0:T(8,128)}), f32[20480,128]{1,0:T(8,128)}) %all-gather.7.cloned.1.call-update) | async-done | bytes 10485776 | tf_op jit(solution)/shard_map/all_gather | solution.py:14
  441.3 1.1 constant_dynamic-slice_fusion.1
  442.4 13.8 %convolution_bitcast_fusion = f32[2560,128]{1,0:T(8,128)} fusion(f32[1280,128]{1,0:T(8,128)S(1)} %constant_dynamic-slice_fusion.1, f32[2560,1280]{1,0:T(8,128)} %param.5), kind=kOutput, calls=%fused_computation.1 | convolution fusion | flops 5033164800 | bytes 15073280 | tf_op jit(solution)/shard_map/dot_general | solution.py:10
  456.2 0.0 reduce-scatter.2.cloned.1.call-update
  456.2 0.0 all-reduce.8.cloned.1.call-start
  456.3 71.3 %reduce-scatter.2.cloned.1.call-done = f32[160,128]{1,0:T(8,128)} async-done(((f32[2560,128]{1,0:T(8,128)}), f32[160,128]{1,0:T(8,128)}) %reduce-scatter.2.cloned.1.call-update) | async-done | bytes 81936 | tf_op jit(solution)/shard_map/reduce_scatter | solution.py:34
  527.6 1.9 fusion.30
  529.5 0.0 all-reduce.8.cloned.1.call-update
  529.6 0.0 all-gather.9.cloned.1.call-start
  529.6 142.0 %all-reduce.8.cloned.1.call-done = f32[128,128]{1,0:T(8,128)} async-done(((f32[128,128]{1,0:T(8,128)}), f32[128,128]{1,0:T(8,128)}) %all-reduce.8.cloned.1.call-update) | async-done | bytes 65552 | tf_op jit(solution)/shard_map/psum | solution.py:37
  671.6 1.8 fusion.6
  673.4 0.0 all-gather.9.cloned.1.call-update
  673.4 0.3 all-gather.11.cloned.1.call-start
  673.7 40.1 %all-gather.9.cloned.1.call-done = f32[2560,128]{1,0:T(8,128)} async-done(((f32[160,128]{1,0:T(8,128)}), f32[2560,128]{1,0:T(8,128)}) %all-gather.9.cloned.1.call-update) | async-done | bytes 1310736 | tf_op jit(solution)/shard_map/all_gather | solution.py:39
  713.9 0.7 copy.10
  714.6 2.2 fusion.17
  716.8 58.3 %all-gather.11.cloned.1.call-done = f32[20480,128]{1,0:T(8,128)} async-done(((f32[2560,128]{1,0:T(8,128)}), f32[20480,128]{1,0:T(8,128)}) %all-gather.11.cloned.1.call-update) | async-done | bytes 10485776 | tf_op jit(solution)/shard_map/all_gather | solution.py:14
  775.1 1.1 constant_dynamic-slice_fusion
  776.2 15.3 %convolution_subtract_fusion = f32[2560,1280]{1,0:T(8,128)} fusion(f32[2560,1280]{1,0:T(8,128)} %param.5, f32[2560,128]{1,0:T(8,128)S(1)} %copy-done.2, f32[2560,128]{1,0:T(8,128)S(1)} %copy-done.1, f32[1280,128]{1,0:T(8,128)S(1)} %constant_dynamic-slice_fusion.1, f32[1280,128]{1,0:T(8,128)S(1)} %constant_dynamic-slice_fusion), kind=kOutput, calls=%fused_computation | convolution fusion | flops 10070589440 | bytes 30146560 | tf_op jit(solution)/shard_map/dot_general | solution.py:10
  (10 shorter events, 0.1 us)
Async XLA Ops:
  7.2 0.9 copy-start
  7.2 147.2 %all-reduce.4.cloned.1.call-start = ((), (), s32[]{:S(2)}) async-start(), calls=%async_computation.1 | async-start | bytes 131072 | tf_op jit(solution)/shard_map/psum | solution.py:21
  9.2 306.1 %all-reduce.6.cloned.1.call-start = ((), (), s32[]{:S(2)}) async-start(), calls=%async_computation.2 | async-start | bytes 131072 | tf_op jit(solution)/shard_map/psum | solution.py:26
  180.4 199.9 %all-gather.5.cloned.1.call-start = ((), (), s32[]{:S(2)}) async-start(), calls=%async_computation.3 | async-start | bytes 1392640 | tf_op jit(solution)/shard_map/all_gather | solution.py:32
  340.9 100.4 %all-gather.7.cloned.1.call-start = ((), (), s32[]{:S(2)}) async-start(), calls=%async_computation.4 | async-start | bytes 11796480 | tf_op jit(solution)/shard_map/all_gather | solution.py:14
  380.3 147.2 %reduce-scatter.2.cloned.1.call-start = ((), (), s32[]{:S(2)}) async-start(), calls=%async_computation.5 | async-start | bytes 1392640 | tf_op jit(solution)/shard_map/reduce_scatter | solution.py:34
  442.4 85.1 %copy-start.3 = (f32[160,128]{1,0:T(8,128)S(1)}, f32[160,128]{1,0:T(8,128)}, u32[]{:S(2)}) copy-start(f32[160,128]{1,0:T(8,128)} %convolution_bitcast_fusion.1) | copy-start | bytes 245764
  456.2 320.0 %copy-start.1 = (f32[2560,128]{1,0:T(8,128)S(1)}, f32[2560,128]{1,0:T(8,128)}, u32[]{:S(2)}) copy-start(f32[2560,128]{1,0:T(8,128)} %all-gather.5.cloned.1.call-done) | copy-start | bytes 3932164
  456.2 215.4 %all-reduce.8.cloned.1.call-start = ((), (), s32[]{:S(2)}) async-start(), calls=%async_computation.6 | async-start | bytes 131072 | tf_op jit(solution)/shard_map/psum | solution.py:37
  529.6 184.3 %all-gather.9.cloned.1.call-start = ((), (), s32[]{:S(2)}) async-start(), calls=%async_computation.7 | async-start | bytes 1392640 | tf_op jit(solution)/shard_map/all_gather | solution.py:39
  673.4 101.6 %all-gather.11.cloned.1.call-start = ((), (), s32[]{:S(2)}) async-start(), calls=%async_computation.8 | async-start | bytes 11796480 | tf_op jit(solution)/shard_map/all_gather | solution.py:14
  713.8 62.4 %copy-start.2 = (f32[2560,128]{1,0:T(8,128)S(1)}, f32[2560,128]{1,0:T(8,128)}, u32[]{:S(2)}) copy-start(f32[2560,128]{1,0:T(8,128)} %all-gather.9.cloned.1.call-done) | copy-start | bytes 3932164
Sparse Core Ops, SparseCore 0:
  13.3 140.9 all-reduce.3
  180.5 134.7 all-reduce.5
  341.0 39.2 all-gather.4
  381.9 59.4 all-gather.6
  456.4 71.1 reduce-scatter.1
  532.8 138.8 all-reduce.7
  674.6 39.2 all-gather.8
  715.6 59.4 all-gather.10
where the time goes:
time: 799 us; the launch traced here: 798 us
  waiting for transfers between devices  692 us (87%)
  other arithmetic  47.6 us (6%)
  matrix products  38.2 us (5%)
  between operations  14.2 us (2%)
    psum x1, waiting for transfers between devices, on_device(): gram_one = lax.psum(matmul(panel_block.T, panel_block), ('row', 'col'))  145 us
    psum x1, waiting for transfers between devices, on_device(): projected = lax.psum(matmul(ortho_basis.T, products), ('row', 'col'))  142 us
    psum x1, waiting for transfers between devices, on_device(): gram_two = lax.psum(matmul(first_q.T, first_q), ('row', 'col'))  135 us
    all_gather x2, waiting for transfers between devices, column_block(): gathered = lax.all_gather(block_rows, 'row', axis=0, tiled=True)  119 us
    reduce_scatter x1, waiting for transfers between devices, on_device(): lax.psum_scatter(matmul(trailing, basis_cols), 'col', scatter_dimension=0...  71.3 us
    all_gather x1, waiting for transfers between devices, on_device(): correction_rows = lax.all_gather(correction, 'col', axis=0, tiled=True)  40.1 us
    all_gather x1, waiting for transfers between devices, on_device(): basis_block = lax.all_gather(ortho_basis, 'col', axis=0, tiled=True)  39.4 us
    dot_general x7, matrix products, matmul(): jnp.dot(first, second, preferred_element_type=jnp.float32, precision=HIGH...  37.2 us
  transfers between devices with their start and end apart: 8, of which 8 were waited for; matrix products, arithmetic and copies ran while one was open for 0% of the time, Pallas kernels for 0%

commit v1 on v0

v1 whole, which is shorter than its diff:
```python
import jax
import jax.numpy as jnp
from jax import lax
from jax.experimental import pallas as pl
from jax.experimental.pallas import tpu as pltpu
from jax.sharding import PartitionSpec as P

HIGHEST = lax.Precision.HIGHEST
MESH = pl.DeviceIdType.MESH
F32 = jnp.float32
BF16 = jnp.bfloat16

ROWS = 8
COLS = 16
NB = 128
SHARD = 160
ROW_BLOCK = SHARD * COLS
COL_BLOCK = SHARD * ROWS


def dot(first, second, contract, precision=HIGHEST):
    return lax.dot_general(
        first, second, (contract, ((), ())), precision=precision, preferred_element_type=F32
    )


def split(value):
    high = value.astype(BF16)
    return high, (value - high.astype(F32)).astype(BF16)


def factor(work, gram, step=32):
    down = lax.broadcasted_iota(jnp.int32, (NB, NB), 0)
    across = lax.broadcasted_iota(jnp.int32, (NB, NB), 1)
    work[:, :NB] = gram
    work[:, NB:] = jnp.where(down == across, 1.0, 0.0)
    sub = lax.broadcasted_iota(jnp.int32, (step, 1), 0)
    for base in range(0, NB, step):
        rows = work[base : base + step, :]
        tall = [
            jnp.broadcast_to(rows[:, base + k : base + k + 1], (step, NB)) for k in range(step)
        ]
        for k in range(step):
            scale = lax.rsqrt(tall[k][k : k + 1, :])
            low = tall[k] * scale
            for m in range(k + 1, step):
                tall[m] = tall[m] - low * low[m : m + 1, :]
            top = rows[k : k + 1, :] * jnp.concatenate([scale, scale], axis=1)
            low = jnp.where(sub > k, low, 0.0)
            rows = jnp.where(sub == k, top, rows - jnp.concatenate([low, low], axis=1) * top)
        work[base : base + step, :] = rows
        if base + step < NB:
            change = dot(rows[:, :NB], rows, ((0,), (0,)))
            work[base + step :, :] = work[base + step :, :] - change[base + step :, :]
    work[:, :NB] = jnp.where(across >= down, work[:, :NB], 0.0)
    work[:, NB:] = jnp.where(across <= down, work[:, NB:], 0.0)


class Exchange:
    def __init__(self, size, me, place, source, target, send_sem, recv_sem):
        self.size, self.me, self.place = size, me, place
        self.source, self.target = source, target
        self.send_sem, self.recv_sem = send_sem, recv_sem

    def each(self, action):
        def body(step, carry):
            action(lax.rem(self.me + step, self.size))
            return carry

        lax.fori_loop(1, self.size, body, 0)

    def copy(self, peer, slot):
        row, col = self.place(peer)
        return pltpu.make_async_remote_copy(
            src_ref=self.source(peer),
            dst_ref=self.target(slot),
            send_sem=self.send_sem.at[peer],
            recv_sem=self.recv_sem.at[slot],
            device_id=(row, col),
            device_id_type=MESH,
        )

    def start(self):
        self.each(lambda peer: self.copy(peer, self.me).start())

    def receive(self):
        self.each(lambda peer: self.copy(peer, peer).wait_recv())

    def finish(self):
        self.each(lambda peer: self.copy(peer, peer).wait_send())


def blocks(ref, size):
    return lambda index: ref.at[pl.ds(pl.multiple_of(index * size, size), size), :]


def panel_kernel(
    trailing_hbm, panel,
    left_x, left_y, right, r_out, first_out,
    a_full, a_high, a_low, p_rows, q_rows, q_wide, p_cols, q_cols,
    y_part, y_buf, y_cols, y_rows,
    g_own, g_buf, g_part, g_all, h_own, h_buf, h_part, h_all,
    work_one, work_two,
    a_sem, send16, recv16, send8, recv8, perm_send, perm_recv,
):
    me_r, me_c = lax.axis_index("row"), lax.axis_index("col")
    in_row = lambda peer: (me_r, peer)
    in_col = lambda peer: (peer, me_c)
    to_cols = (lax.rem(me_c, 8), 2 * me_r + me_c // 8)
    to_rows = (me_c // 2, 8 * lax.rem(me_c, 2) + me_r)
    fixed = jnp.logical_and(to_cols[0] == me_r, to_cols[1] == me_c)

    load = pltpu.make_async_copy(trailing_hbm, a_full, a_sem)
    load.start()

    barrier = pltpu.get_barrier_semaphore()

    def greet(size, me, place):
        def body(step, carry):
            pl.semaphore_signal(
                barrier, inc=1, device_id=place(lax.rem(me + step, size)), device_id_type=MESH
            )
            return carry

        lax.fori_loop(1, size, body, 0)

    greet(COLS, me_c, in_row)
    greet(ROWS, me_r, in_col)

    @pl.when(jnp.logical_not(fixed))
    def _():
        pl.semaphore_signal(barrier, inc=1, device_id=to_cols, device_id_type=MESH)
        pl.semaphore_signal(barrier, inc=1, device_id=to_rows, device_id_type=MESH)

    g_own[...] = dot(panel[...], panel[...], ((0,), (0,)))
    my_rows = pl.ds(pl.multiple_of(me_r * SHARD, SHARD), SHARD)
    my_cols = pl.ds(pl.multiple_of(me_c * SHARD, SHARD), SHARD)
    p_rows[my_cols, :] = panel[...]

    pl.semaphore_wait(barrier, jnp.where(fixed, COLS + ROWS - 2, COLS + ROWS))

    def permute(source, target, place, slot, sem):
        return pltpu.make_async_remote_copy(
            src_ref=source, dst_ref=blocks(target, SHARD)(slot),
            send_sem=perm_send.at[sem], recv_sem=perm_recv.at[sem],
            device_id=place, device_id_type=MESH,
        )

    def total(buf, own, count):
        value = own
        for k in range(count):
            part = buf[k * 8 : k * 8 + 8, :]
            value = part if k == 0 else value + part
        return value

    eight = lambda index: pl.ds(pl.multiple_of(index * 8, 8), 8)

    def summed(own, buf, part, full, sem):
        scatter = Exchange(
            COLS, me_c, in_row, blocks(own, 8), blocks(buf, 8), send16.at[sem], recv16.at[sem]
        )
        share = Exchange(
            ROWS, me_r, in_col, lambda peer: blocks(part, 8)(me_r), blocks(part, 8),
            send8.at[sem], recv8.at[sem],
        )
        gather = Exchange(
            COLS, me_c, in_row, lambda peer: blocks(full, 8)(me_c), blocks(full, 8),
            send16.at[sem + 1], recv16.at[sem + 1],
        )

        def one():
            buf[eight(me_c), :] = own[eight(me_c), :]
            scatter.start()

        def two():
            scatter.receive()
            part[eight(me_r), :] = total(buf, None, COLS)
            share.start()

        def three():
            share.receive()
            full[eight(me_c), :] = total(part, None, ROWS)
            gather.start()

        def four():
            gather.receive()

        def finish():
            scatter.finish()
            share.finish()
            gather.finish()

        return one, two, three, four, finish

    one, two, three, four, gram_finish = summed(g_own, g_buf, g_part, g_all, 0)
    one()

    @pl.when(jnp.logical_not(fixed))
    def _():
        permute(panel, p_cols, to_cols, to_cols[0], 0).start()

    @pl.when(fixed)
    def _():
        p_cols[my_rows, :] = panel[...]

    two()

    @pl.when(jnp.logical_not(fixed))
    def _():
        permute(panel, p_cols, to_cols, me_r, 0).wait_recv()

    three()
    panel_rows = Exchange(
        COLS, me_c, in_row, lambda peer: panel, blocks(p_rows, SHARD), send16.at[4], recv16.at[4]
    )
    panel_rows.start()
    panel_cols = Exchange(
        ROWS, me_r, in_col, lambda peer: blocks(p_cols, SHARD)(me_r), blocks(p_cols, SHARD),
        send8.at[4], recv8.at[4],
    )
    panel_cols.start()
    load.wait()

    def split_rows(index, carry):
        rows = pl.ds(pl.multiple_of(index * 64, 64), 64)
        a_high[rows, :], a_low[rows, :] = split(a_full[rows, :])
        return carry

    lax.fori_loop(0, ROW_BLOCK // 64, split_rows, 0)
    four()
    factor(work_one, g_all[...])
    first_out[...] = work_one[:, :NB]
    inverse = work_one[:, NB:]

    panel_rows.receive()

    def basis_rows(index, carry):
        rows = pl.ds(pl.multiple_of(index * 256, 256), 256)
        value = dot(p_rows[rows, :], inverse, ((1,), (1,)))
        q_rows[rows, :] = value
        high, low = split(value.T)
        q_wide[:NB, rows] = high
        q_wide[NB:, rows] = low
        return carry

    lax.fori_loop(0, ROW_BLOCK // 256, basis_rows, 0)
    panel_cols.receive()

    def basis_cols(index, carry):
        rows = pl.ds(pl.multiple_of(index * 256, 256), 256)
        q_cols[rows, :] = dot(p_cols[rows, :], inverse, ((1,), (1,)))
        return carry

    lax.fori_loop(0, COL_BLOCK // 256, basis_cols, 0)

    def products(index, carry):
        cols = pl.ds(pl.multiple_of(index * 256, 256), 256)
        wide = dot(q_wide[...], a_high[:, cols], ((1,), (0,)), None)
        value = wide[:NB, :] + wide[NB:, :] + dot(q_wide[:NB, :], a_low[:, cols], ((1,), (0,)), None)
        y_part[cols, :] = value.T
        return carry

    lax.fori_loop(0, COL_BLOCK // 256, products, 0)

    y_scatter = Exchange(
        ROWS, me_r, in_col, blocks(y_part, SHARD), blocks(y_buf, SHARD), send8.at[5], recv8.at[5]
    )
    y_scatter.start()
    y_buf[my_rows, :] = y_part[my_rows, :]
    mine = q_rows[my_cols, :]
    h_own[:, :NB] = dot(mine, mine, ((0,), (0,)))
    h_own[:, NB:] = dot(q_cols[...], y_part[...], ((0,), (0,)))
    one, two, three, four, more_finish = summed(h_own, h_buf, h_part, h_all, 2)
    one()
    y_scatter.receive()
    value = y_buf[:SHARD, :]
    for k in range(1, ROWS):
        value = value + y_buf[k * SHARD : (k + 1) * SHARD, :]
    y_cols[my_rows, :] = value
    y_shard = blocks(y_cols, SHARD)(me_r)

    @pl.when(jnp.logical_not(fixed))
    def _():
        permute(y_shard, y_rows, to_rows, to_rows[1], 1).start()

    @pl.when(fixed)
    def _():
        y_rows[my_cols, :] = y_cols[my_rows, :]

    y_columns = Exchange(
        ROWS, me_r, in_col, lambda peer: y_shard, blocks(y_cols, SHARD), send8.at[6], recv8.at[6]
    )
    y_columns.start()
    two()

    @pl.when(jnp.logical_not(fixed))
    def _():
        permute(y_shard, y_rows, to_rows, me_c, 1).wait_recv()

    three()
    y_gather = Exchange(
        COLS, me_c, in_row, lambda peer: blocks(y_rows, SHARD)(me_c), blocks(y_rows, SHARD),
        send16.at[5], recv16.at[5],
    )
    y_gather.start()
    four()

    factor(work_two, h_all[:, :NB])
    r_out[...] = dot(work_two[:, :NB], work_one[:, :NB], ((1,), (0,)))
    second = work_two[:, NB:]
    gram_inverse = dot(second, second, ((0,), (0,)))
    core = 4.0 * h_all[:, NB:]

    def finish_x(index, carry):
        rows = pl.ds(pl.multiple_of(index * 256, 256), 256)
        left_x[rows, :] = dot(q_rows[rows, :], gram_inverse, ((1,), (0,)))
        return carry

    lax.fori_loop(0, ROW_BLOCK // 256, finish_x, 0)
    y_columns.receive()

    def finish_right(index, carry):
        rows = pl.ds(pl.multiple_of(index * 256, 256), 256)
        x_tile = dot(q_cols[rows, :], gram_inverse, ((1,), (0,)))
        right[rows, :NB] = 2.0 * y_cols[rows, :] - dot(x_tile, core, ((1,), (0,)))
        right[rows, NB:] = 2.0 * x_tile
        return carry

    lax.fori_loop(0, COL_BLOCK // 256, finish_right, 0)
    y_gather.receive()
    left_y[...] = y_rows[...]

    gram_finish()
    panel_rows.finish()
    panel_cols.finish()
    y_scatter.finish()
    more_finish()
    y_columns.finish()
    y_gather.finish()

    @pl.when(jnp.logical_not(fixed))
    def _():
        permute(panel, p_cols, to_cols, to_cols[0], 0).wait_send()
        permute(y_shard, y_rows, to_rows, to_rows[1], 1).wait_send()


def panel_call(trailing, panel_block):
    vmem = pl.BlockSpec(memory_space=pltpu.VMEM)
    shape = lambda *dims: jax.ShapeDtypeStruct(dims, F32)
    tall, wide = (ROW_BLOCK, NB), (COL_BLOCK, NB)
    f32 = lambda *dims: pltpu.VMEM(dims, F32)
    bf16 = lambda *dims: pltpu.VMEM(dims, BF16)
    dma = lambda *dims: pltpu.SemaphoreType.DMA(dims)
    return pl.pallas_call(
        panel_kernel,
        out_shape=[
            shape(*tall), shape(*tall), shape(COL_BLOCK, 2 * NB), shape(NB, NB), shape(NB, NB)
        ],
        in_specs=[pl.BlockSpec(memory_space=pl.ANY), vmem],
        out_specs=[vmem] * 5,
        scratch_shapes=[
            f32(ROW_BLOCK, COL_BLOCK), bf16(ROW_BLOCK, COL_BLOCK), bf16(ROW_BLOCK, COL_BLOCK),
            f32(*tall), f32(*tall), bf16(2 * NB, ROW_BLOCK), f32(*wide), f32(*wide),
            f32(*wide), f32(*wide), f32(*wide), f32(*tall),
            f32(NB, NB), f32(NB, NB), f32(8 * ROWS, NB), f32(NB, NB),
            f32(NB, 2 * NB), f32(NB, 2 * NB), f32(8 * ROWS, 2 * NB), f32(NB, 2 * NB),
            f32(NB, 2 * NB), f32(NB, 2 * NB),
            pltpu.SemaphoreType.DMA, dma(6, COLS), dma(6, COLS), dma(7, ROWS), dma(7, ROWS),
            dma(2), dma(2),
        ],
        compiler_params=pltpu.CompilerParams(
            collective_id=0, has_side_effects=True, vmem_limit_bytes=56 * 1024 * 1024
        ),
        name="panel",
    )(trailing, panel_block)


def on_device(trailing, panel_block):
    left_x, left_y, right, r_factor, first_factor = panel_call(trailing, panel_block)
    left = jnp.concatenate([left_x, left_y], axis=1)
    change = jnp.dot(left, right.T, preferred_element_type=F32, precision=lax.Precision.HIGH)
    return trailing - change, r_factor, first_factor


def solution(mesh):
    in_specs = (P("row", "col"), P(("row", "col"), None))
    out_specs = (P("row", "col"), P(), P())
    return jax.shard_map(
        on_device, mesh=mesh, in_specs=in_specs, out_specs=out_specs, check_vma=False
    )
```

time: 799 us -> 115 us (0.14)
  waiting for transfers between devices: 692 us -> 0 us
  Pallas kernels: 0 us -> 101 us
  other arithmetic: 47.6 us -> 0 us
  matrix products: 38.2 us -> 12.2 us
  between operations: 14.2 us -> 0.66 us
    psum x3 -> x0, waiting for transfers between devices: 422 us -> none  [the longest x1 145 us: on_device(): gram_one = lax.psum(matmul(panel_block.T, panel_block), ('row', 'col'))]
    all_gather x4 -> x0, waiting for transfers between devices: 199 us -> none  [the longest x2 119 us: column_block(): gathered = lax.all_gather(block_rows, 'row', axis=0, tiled=True)]
    pallas_call x0 -> x1, Pallas kernels: none -> 101 us  [panel_call(): pl.pallas_call(panel_kernel, out_shape=[shape(*tall), shape(*tall), shape...]
    reduce_scatter x1 -> x0, waiting for transfers between devices: 71.3 us -> none  [on_device(): lax.psum_scatter(matmul(trailing, basis_cols), 'col', scatter_dimension=0...]
    another operation x9 -> x0, other arithmetic: 45.2 us -> none  [the longest x3 12.5 us: on_device(): low_two = jnp.linalg.cholesky(gram_two)]
    dot_general x7 -> x1, matrix products: 37.2 us -> 12.2 us  [on_device(): jnp.dot(left, right.T, preferred_element_type=F32, precision=lax.Precisio...]
  transfers between devices with their start and end apart: 8 -> 0, of which waited for: 8 -> 0; matrix products, arithmetic and copies ran while one was open for 0% -> 0% of each run, Pallas kernels for 0% -> 0%
where the time goes in v1:
time: 115 us
  Pallas kernels  101 us (88%)
  matrix products  12.2 us (11%)
  local copies, waits for them, and re-layouts  1.27 us (1%)
    pallas_call x1, Pallas kernels, panel_call(): pl.pallas_call(panel_kernel, out_shape=[shape(*tall), shape(*tall), shape...  101 us
    dot_general x1, matrix products, on_device(): jnp.dot(left, right.T, preferred_element_type=F32, precision=lax.Precisio...  12.2 us

profile of v1, /device:TPU:1, one launch (start us, length us, event | category | flops | bytes accessed | tf_op | source)
XLA Modules:
  0.0 114.8 jit_solution(1829358317237335471)
XLA Ops:
  0.6 100.7 %panel.2 = (f32[2560,128]{1,0:T(8,128)}, f32[2560,128]{1,0:T(8,128)}, f32[1280,256]{1,0:T(8,128)}, f32[128,128]{1,0:T(8,128)}, f32[128,128]{1,0:T(8,128)}) custom-call(f32[2560,1280]{1,0:T(8,128)} %trailing_hbm.1, f32[160,128]{1,0:T(8,128)} %panel.3), custom_call_target="tpu_custom_call" | custom-call | tf_op jit(solution)/shard_map/panel/pallas_call | solution.py:354
  101.3 0.0 copy-start.1
  101.3 0.0 copy-start
  101.3 12.2 %convolution_subtract_fusion = f32[2560,1280]{1,0:T(8,128)} fusion(f32[2560,1280]{1,0:T(8,128)} %trailing_hbm.1, f32[1280,256]{1,0:T(8,128)} %get-tuple-element.10, f32[2560,128]{1,0:T(8,128)} %get-tuple-element.9, f32[2560,128]{1,0:T(8,128)} %get-tuple-element.8), kind=kOutput, calls=%fused_computation | convolution fusion | flops 5037096960 | bytes 30146560 | tf_op jit(solution)/shard_map/dot_general | solution.py:381
  113.6 0.0 copy-done.1
  113.6 0.6 copy.7
  114.2 0.0 copy-done
  114.2 0.6 copy.8
Async XLA Ops:
  101.3 12.2 %copy-start.1 = (f32[128,128]{1,0:T(8,128)S(1)}, f32[128,128]{1,0:T(8,128)}, u32[]{:S(2)}) copy-start(f32[128,128]{1,0:T(8,128)} %get-tuple-element.17) | copy-start | bytes 196612
  101.3 12.9 %copy-start = (f32[128,128]{1,0:T(8,128)S(1)}, f32[128,128]{1,0:T(8,128)}, u32[]{:S(2)}) copy-start(f32[128,128]{1,0:T(8,128)} %get-tuple-element.18) | copy-start | bytes 196612

commit v2 on v1

v2 whole, which is shorter than its diff:
```python
import jax
import jax.numpy as jnp
from jax import lax
from jax.experimental import pallas as pl
from jax.experimental.pallas import tpu as pltpu
from jax.sharding import PartitionSpec as P

HIGHEST = lax.Precision.HIGHEST
MESH = pl.DeviceIdType.MESH
F32 = jnp.float32
BF16 = jnp.bfloat16

ROWS = 8
COLS = 16
SIDE = 4
NB = 128
SHARD = 160
HALF = 80
ROW_BLOCK = SHARD * COLS
COL_BLOCK = SHARD * ROWS
TILE = 256


def dot(first, second, contract, precision=HIGHEST):
    return lax.dot_general(
        first, second, (contract, ((), ())), precision=precision, preferred_element_type=F32
    )


def split(value):
    high = value.astype(BF16)
    return high, (value - high.astype(F32)).astype(BF16)


def factor(work, gram, step=32):
    down = lax.broadcasted_iota(jnp.int32, (NB, NB), 0)
    across = lax.broadcasted_iota(jnp.int32, (NB, NB), 1)
    work[:, :NB] = gram
    work[:, NB:] = jnp.where(down == across, 1.0, 0.0)
    sub = lax.broadcasted_iota(jnp.int32, (step, 1), 0)
    for base in range(0, NB, step):
        rows = work[base : base + step, :]
        tall = [
            jnp.broadcast_to(rows[:, base + k : base + k + 1], (step, NB)) for k in range(step)
        ]
        for k in range(step):
            scale = lax.rsqrt(tall[k][k : k + 1, :])
            low = tall[k] * scale
            for m in range(k + 1, step):
                tall[m] = tall[m] - low * low[m : m + 1, :]
            top = rows[k : k + 1, :] * jnp.concatenate([scale, scale], axis=1)
            low = jnp.where(sub > k, low, 0.0)
            rows = jnp.where(sub == k, top, rows - jnp.concatenate([low, low], axis=1) * top)
        work[base : base + step, :] = rows
        if base + step < NB:
            change = dot(rows[:, :NB], rows, ((0,), (0,)))
            work[base + step :, :] = work[base + step :, :] - change[base + step :, :]
    work[:, :NB] = jnp.where(across >= down, work[:, :NB], 0.0)
    work[:, NB:] = jnp.where(across <= down, work[:, NB:], 0.0)


class Exchange:
    def __init__(self, size, me, place, source, target, send_sem, recv_sem):
        self.size, self.me, self.place = size, me, place
        self.source, self.target = source, target
        self.send_sem, self.recv_sem = send_sem, recv_sem

    def each(self, action):
        def body(step, carry):
            action(lax.rem(self.me + step, self.size))
            return carry

        lax.fori_loop(1, self.size, body, 0)

    def copy(self, peer, slot):
        return pltpu.make_async_remote_copy(
            src_ref=self.source(peer),
            dst_ref=self.target(slot),
            send_sem=self.send_sem.at[peer],
            recv_sem=self.recv_sem.at[slot],
            device_id=self.place(peer),
            device_id_type=MESH,
        )

    def start(self):
        self.each(lambda peer: self.copy(peer, self.me).start())

    def receive(self):
        self.each(lambda peer: self.copy(peer, peer).wait_recv())

    def finish(self):
        self.each(lambda peer: self.copy(peer, peer).wait_send())


class Swap:
    def __init__(self, apart, place, source, target, there, here, send_sem, recv_sem):
        self.apart, self.here, self.source, self.target = apart, here, source, target
        self.copy = lambda slot: pltpu.make_async_remote_copy(
            src_ref=source, dst_ref=target(slot), send_sem=send_sem, recv_sem=recv_sem,
            device_id=place, device_id_type=MESH,
        )
        self.there = there

    def start(self):
        @pl.when(self.apart)
        def _():
            self.copy(self.there).start()

        @pl.when(jnp.logical_not(self.apart))
        def _():
            self.target(self.here)[...] = self.source[...]

    def receive(self):
        @pl.when(self.apart)
        def _():
            self.copy(self.here).wait_recv()

    def finish(self):
        @pl.when(self.apart)
        def _():
            self.copy(self.there).wait_send()


def eights(ref):
    return lambda index: ref.at[pl.ds(pl.multiple_of(index * 8, 8), 8), :]


def panel_kernel(
    trailing_hbm, panel,
    left_high, left_low, right_high, right_low, r_out, first_out,
    a_full, a_high, a_low, p_rows, q_rows, q_wide, p_cols, q_cols,
    y_part, y_mate, y_half, y_ring, y_cols, y_rows,
    g_own, g_buf, g_part, g_all, h_own, h_buf, h_part, h_all,
    work_one, work_two,
    a_sem, plane_send, plane_recv, axis_send, axis_recv, ring_send, ring_recv, one_send, one_recv,
):
    me_r, me_c = lax.axis_index("row"), lax.axis_index("col")
    z, core = me_r // 2, lax.rem(me_r, 2)
    y, x = me_c // SIDE, lax.rem(me_c, SIDE)
    in_plane = lambda peer: (me_r, peer)
    in_axis = lambda peer: (peer, me_c)
    in_x = lambda peer: (me_r, y * SIDE + peer)
    in_y = lambda peer: (me_r, peer * SIDE + x)
    in_z = lambda peer: (2 * peer + core, me_c)
    mate = (2 * z + 1 - core, me_c)
    out_r, out_c = lax.rem(me_c, ROWS), 2 * me_r + me_c // ROWS
    in_r, in_c = me_c // 2, ROWS * lax.rem(me_c, 2) + me_r
    apart = jnp.logical_not(jnp.logical_and(out_r == me_r, out_c == me_c))
    straight = core == x // 2
    turn_r = 2 * y + jnp.where(straight, core, 1 - core)
    turn_c = z * SIDE + jnp.where(straight, x, SIDE - 1 - x)
    turned = jnp.logical_not(jnp.logical_and(straight, y == z))

    load = pltpu.make_async_copy(trailing_hbm, a_full, a_sem)
    load.start()

    barrier = pltpu.get_barrier_semaphore()

    def signal(place):
        pl.semaphore_signal(barrier, inc=1, device_id=place, device_id_type=MESH)

    def greet(size, me, place):
        def body(step, carry):
            signal(place(lax.rem(me + step, size)))
            return carry

        lax.fori_loop(1, size, body, 0)

    greet(COLS, me_c, in_plane)
    greet(ROWS, me_r, in_axis)

    @pl.when(apart)
    def _():
        signal((out_r, out_c))
        signal((in_r, in_c))

    @pl.when(turned)
    def _():
        signal((turn_r, turn_c))

    g_own[...] = dot(panel[...], panel[...], ((0,), (0,)))
    for half in range(2):
        p_rows[y, x, half] = panel[half * HALF : (half + 1) * HALF, :]
    pl.semaphore_wait(
        barrier, COLS + ROWS - 2 + jnp.where(apart, 2, 0) + jnp.where(turned, 1, 0)
    )

    def summed(own, buf, part, full, sem):
        scatter = Exchange(
            COLS, me_c, in_plane, eights(own), eights(buf),
            plane_send.at[sem], plane_recv.at[sem],
        )
        share = Exchange(
            ROWS, me_r, in_axis, lambda peer: eights(part)(me_r), eights(part),
            axis_send.at[sem], axis_recv.at[sem],
        )
        gather = Exchange(
            COLS, me_c, in_plane, lambda peer: eights(full)(me_c), eights(full),
            plane_send.at[sem + 2], plane_recv.at[sem + 2],
        )

        def total(source, count):
            value = source[:8, :]
            for k in range(1, count):
                value = value + source[k * 8 : k * 8 + 8, :]
            return value

        def one():
            eights(buf)(me_c)[...] = eights(own)(me_c)[...]
            scatter.start()

        def two():
            scatter.receive()
            eights(part)(me_r)[...] = total(buf, COLS)
            share.start()

        def three():
            share.receive()
            eights(full)(me_c)[...] = total(part, ROWS)
            gather.start()

        def finish():
            scatter.finish()
            share.finish()
            gather.finish()

        return one, two, three, gather.receive, finish

    def ring(place, me, source, target, sem):
        return Exchange(SIDE, me, place, source, target, ring_send.at[sem], ring_recv.at[sem])

    def plane_gather(rows, sem):
        first = (
            ring(in_y, y, lambda peer: rows.at[y, x, 0], lambda slot: rows.at[slot, x, 0], sem),
            ring(in_x, x, lambda peer: rows.at[y, x, 1], lambda slot: rows.at[y, slot, 1], sem + 1),
        )
        second = (
            ring(in_x, x, lambda peer: rows.at[:, x, 0], lambda slot: rows.at[:, slot, 0], sem + 2),
            ring(in_y, y, lambda peer: rows.at[y, :, 1], lambda slot: rows.at[slot, :, 1], sem + 3),
        )
        return first, second

    def start(pair):
        for item in pair:
            item.start()

    def receive(pair):
        for item in pair:
            item.receive()

    def axis_gather(cols, sem, mate_sem):
        along = ring(
            in_z, z, lambda peer: cols.at[z, core], lambda slot: cols.at[slot, core], sem
        )
        across = Swap(
            True, mate, cols.at[:, core], lambda slot: cols.at[:, slot], core, 1 - core,
            one_send.at[mate_sem], one_recv.at[mate_sem],
        )
        return along, across

    one, two, three, gram_all, gram_finish = summed(g_own, g_buf, g_part, g_all, 0)
    p_first, p_second = plane_gather(p_rows, 0)
    p_swap = Swap(
        apart, (out_r, out_c), panel, lambda slot: p_cols.at[slot // 2, lax.rem(slot, 2)],
        out_r, me_r, one_send.at[0], one_recv.at[0],
    )
    p_along, p_across = axis_gather(p_cols, 8, 1)
    one()
    start(p_first)
    two()
    p_swap.start()
    three()
    receive(p_first)
    start(p_second)
    load.wait()

    def split_rows(index, carry):
        rows = pl.ds(pl.multiple_of(index * 64, 64), 64)
        a_high[rows, :], a_low[rows, :] = split(a_full[rows, :])
        return carry

    lax.fori_loop(0, ROW_BLOCK // 64, split_rows, 0)
    gram_all()
    p_swap.receive()
    p_along.start()
    factor(work_one, g_all[...])
    first_out[...] = work_one[:, :NB]
    inverse = work_one[:, NB:]
    p_along.receive()
    p_across.start()
    receive(p_second)

    def basis_rows(index, carry):
        wide = SIDE * SHARD
        rows = pl.ds(pl.multiple_of(index * wide, wide), wide)
        value = dot(p_rows[index].reshape(wide, NB), inverse, ((1,), (1,)))
        q_rows[rows, :] = value
        high, low = split(value.T)
        q_wide[:NB, rows] = high
        q_wide[NB:, rows] = low
        return carry

    lax.fori_loop(0, SIDE, basis_rows, 0)

    def products(index, carry):
        cols = pl.ds(pl.multiple_of(index * TILE, TILE), TILE)
        wide = dot(q_wide[...], a_high[:, cols], ((1,), (0,)), None)
        value = wide[:NB, :] + wide[NB:, :]
        value = value + dot(q_wide[:NB, :], a_low[:, cols], ((1,), (0,)), None)
        y_part[cols, :] = value.T
        return carry

    lax.fori_loop(0, COL_BLOCK // TILE, products, 0)

    piece = lambda place, k: pl.ds(pl.multiple_of((2 * place + k) * SHARD, SHARD), SHARD)
    y_pair = [
        pltpu.make_async_remote_copy(
            src_ref=y_part.at[piece(k, 1 - core), :], dst_ref=y_mate.at[k],
            send_sem=one_send.at[4 + k], recv_sem=one_recv.at[4 + k],
            device_id=mate, device_id_type=MESH,
        )
        for k in range(SIDE)
    ]
    for item in y_pair:
        item.start()

    def basis_cols(index, carry):
        rows = pl.ds(pl.multiple_of(index * 2 * SHARD, 2 * SHARD), 2 * SHARD)
        q_cols[rows, :] = dot(p_cols[index].reshape(2 * SHARD, NB), inverse, ((1,), (1,)))
        return carry

    for k in range(SIDE):
        y_pair[k].wait_recv()
        y_half[k] = y_part[piece(k, core), :] + y_mate[k]
    y_along = ring(in_z, z, lambda peer: y_half.at[peer], lambda slot: y_ring.at[slot], 9)
    y_along.start()
    p_across.receive()
    lax.fori_loop(0, SIDE, basis_cols, 0)
    mine = q_rows[pl.ds(pl.multiple_of(me_c * SHARD, SHARD), SHARD), :]
    h_own[:, :NB] = dot(mine, mine, ((0,), (0,)))
    h_own[:, NB:] = dot(q_cols[...], y_part[...], ((0,), (0,)))
    one, two, three, more_all, more_finish = summed(h_own, h_buf, h_part, h_all, 1)
    one()
    y_ring[z] = y_half[z]
    y_along.receive()
    y_cols[z, core] = y_ring[0] + y_ring[1] + (y_ring[2] + y_ring[3])
    y_first, y_second = plane_gather(y_rows, 4)
    y_swaps = [
        Swap(
            turned, (turn_r, turn_c), y_cols.at[z, core, pl.ds(half * HALF, HALF)],
            lambda slot, half=half: y_rows.at[slot // SIDE, lax.rem(slot, SIDE), half],
            turn_c, me_c, one_send.at[2 + half], one_recv.at[2 + half],
        )
        for half in range(2)
    ]
    y_columns, y_across = axis_gather(y_cols, 10, 8)
    start(y_swaps)
    two()
    y_columns.start()
    receive(y_swaps)
    start(y_first)
    three()
    receive(y_first)
    start(y_second)
    y_columns.receive()
    y_across.start()
    more_all()

    factor(work_two, h_all[:, :NB])
    r_out[...] = dot(work_two[:, :NB], work_one[:, :NB], ((1,), (0,)))
    second = work_two[:, NB:]
    gram_inverse = dot(second, second, ((0,), (0,)))
    center = 4.0 * h_all[:, NB:]

    def finish_x(index, carry):
        rows = pl.ds(pl.multiple_of(index * TILE, TILE), TILE)
        high, low = split(dot(q_rows[rows, :], gram_inverse, ((1,), (0,))))
        left_high[rows, :NB] = high
        left_low[rows, :NB] = low
        return carry

    lax.fori_loop(0, ROW_BLOCK // TILE, finish_x, 0)
    y_across.receive()

    def finish_right(index, carry):
        rows = pl.ds(pl.multiple_of(index * 2 * SHARD, 2 * SHARD), 2 * SHARD)
        x_tile = dot(q_cols[rows, :], gram_inverse, ((1,), (0,)))
        mixed = 2.0 * y_cols[index].reshape(2 * SHARD, NB) - dot(x_tile, center, ((1,), (0,)))
        right_high[rows, :NB], right_low[rows, :NB] = split(mixed)
        right_high[rows, NB:], right_low[rows, NB:] = split(2.0 * x_tile)
        return carry

    lax.fori_loop(0, SIDE, finish_right, 0)
    receive(y_second)

    def finish_y(index, carry):
        down, over = index // SIDE, lax.rem(index, SIDE)
        same = over // 2 == core
        source_x = jnp.where(same, over, SIDE - 1 - over)
        source_core = jnp.where(same, core, 1 - core)
        rank = lax.rem(source_x, 2) * ROWS + 2 * down + source_core
        rows = pl.ds(pl.multiple_of(rank * SHARD, SHARD), SHARD)
        left_high[rows, NB:], left_low[rows, NB:] = split(y_rows[down, over].reshape(SHARD, NB))
        return carry

    lax.fori_loop(0, COLS, finish_y, 0)

    gram_finish()
    more_finish()
    for item in (*p_first, *p_second, p_swap, p_along, p_across, y_along):
        item.finish()
    for item in (*y_swaps, *y_first, *y_second, y_columns, y_across):
        item.finish()
    for item in y_pair:
        item.wait_send()


def panel_call(trailing, panel_block):
    vmem = pl.BlockSpec(memory_space=pltpu.VMEM)
    f32 = lambda *dims: pltpu.VMEM(dims, F32)
    bf16 = lambda *dims: pltpu.VMEM(dims, BF16)
    dma = lambda *dims: pltpu.SemaphoreType.DMA(dims)
    left = jax.ShapeDtypeStruct((ROW_BLOCK, 2 * NB), BF16)
    right = jax.ShapeDtypeStruct((COL_BLOCK, 2 * NB), BF16)
    small = jax.ShapeDtypeStruct((NB, NB), F32)
    plane = f32(SIDE, SIDE, 2, HALF, NB)
    axis = f32(SIDE, 2, SHARD, NB)
    ring = f32(SIDE, SHARD, NB)
    return pl.pallas_call(
        panel_kernel,
        out_shape=[left, left, right, right, small, small],
        in_specs=[pl.BlockSpec(memory_space=pl.ANY), vmem],
        out_specs=[vmem] * 6,
        scratch_shapes=[
            f32(ROW_BLOCK, COL_BLOCK), bf16(ROW_BLOCK, COL_BLOCK), bf16(ROW_BLOCK, COL_BLOCK),
            plane, f32(ROW_BLOCK, NB), bf16(2 * NB, ROW_BLOCK), axis, f32(COL_BLOCK, NB),
            f32(COL_BLOCK, NB), ring, ring, ring, axis, plane,
            f32(NB, NB), f32(NB, NB), f32(8 * ROWS, NB), f32(NB, NB),
            f32(NB, 2 * NB), f32(NB, 2 * NB), f32(8 * ROWS, 2 * NB), f32(NB, 2 * NB),
            f32(NB, 2 * NB), f32(NB, 2 * NB),
            pltpu.SemaphoreType.DMA, dma(4, COLS), dma(4, COLS), dma(2, ROWS), dma(2, ROWS),
            dma(11, SIDE), dma(11, SIDE), dma(9), dma(9),
        ],
        compiler_params=pltpu.CompilerParams(
            collective_id=0, has_side_effects=True, vmem_limit_bytes=56 * 1024 * 1024
        ),
        name="panel",
    )(trailing, panel_block)


def update_kernel(
    trailing, left_high, left_low, right_high, right_low, r_in, first_in, out, r_out, first_out
):
    change = dot(left_high[...], right_high[...], ((1,), (1,)), None)
    change = change + dot(left_high[...], right_low[...], ((1,), (1,)), None)
    change = change + dot(left_low[...], right_high[...], ((1,), (1,)), None)
    out[...] = trailing[...] - change

    @pl.when(pl.program_id(0) == 0)
    def _():
        r_out[...] = r_in[...]
        first_out[...] = first_in[...]


def update_call(trailing, left_high, left_low, right_high, right_low, r_factor, first_factor):
    tile = pl.BlockSpec((TILE, COL_BLOCK), lambda i: (i, 0))
    left = pl.BlockSpec((TILE, 2 * NB), lambda i: (i, 0))
    right = pl.BlockSpec((COL_BLOCK, 2 * NB), lambda i: (0, 0))
    small = pl.BlockSpec((NB, NB), lambda i: (0, 0))
    return pl.pallas_call(
        update_kernel,
        grid=(ROW_BLOCK // TILE,),
        out_shape=[
            jax.ShapeDtypeStruct((ROW_BLOCK, COL_BLOCK), F32),
            jax.ShapeDtypeStruct((NB, NB), F32),
            jax.ShapeDtypeStruct((NB, NB), F32),
        ],
        in_specs=[tile, left, left, right, right, small, small],
        out_specs=[tile, small, small],
        compiler_params=pltpu.CompilerParams(
            dimension_semantics=("arbitrary",), vmem_limit_bytes=40 * 1024 * 1024
        ),
        name="update",
    )(trailing, left_high, left_low, right_high, right_low, r_factor, first_factor)


def on_device(trailing, panel_block):
    pieces = panel_call(trailing, panel_block)
    return tuple(update_call(trailing, *pieces))


def solution(mesh):
    in_specs = (P("row", "col"), P(("row", "col"), None))
    out_specs = (P("row", "col"), P(), P())
    return jax.shard_map(
        on_device, mesh=mesh, in_specs=in_specs, out_specs=out_specs, check_vma=False
    )
```

time: 115 us -> 97.2 us (0.85)
  the two profiles are of different devices: /device:TPU:1 before, /device:TPU:6 now
where the time goes in v2:
time: 97.2 us; the launch traced here: 96.6 us
  Pallas kernels  89.5 us (92%)
  local copies, waits for them, and re-layouts  6.48 us (7%)
    pallas_call x1, Pallas kernels, panel_call(): pl.pallas_call(panel_kernel, out_shape=[left, left, right, right, small,...  74.2 us
    pallas_call x1, Pallas kernels, update_call(): pl.pallas_call(update_kernel, grid=(ROW_BLOCK // TILE,), out_shape=[jax.S...  15.3 us
    unnamed x12, local copies, waits for them, and re-layouts  6.48 us

profile of v2, /device:TPU:6, one launch (start us, length us, event | category | flops | bytes accessed | tf_op | source)
XLA Modules:
  0.0 96.6 jit_solution(4216877644446374976)
XLA Ops:
  0.6 74.2 %panel.2 = (bf16[2560,256]{1,0:T(8,128)(2,1)}, bf16[2560,256]{1,0:T(8,128)(2,1)}, bf16[1280,256]{1,0:T(8,128)(2,1)}, bf16[1280,256]{1,0:T(8,128)(2,1)}, f32[128,128]{1,0:T(8,128)}, /*index=5*/f32[128,128]{1,0:T(8,128)}) custom-call(f32[2560,1280]{1,0:T(8,128)} %trailing.1, f32[160,128]{1,0:T(8,128)} %panel.3), custom_call_target="tpu_custom_call" | custom-call | tf_op jit(solution)/shard_map/panel/pallas_call | solution.py:429
  74.8 0.0 copy-start
  74.8 1.3 %copy-done = bf16[2560,256]{1,0:T(8,128)(2,1)S(1)} copy-done((bf16[2560,256]{1,0:T(8,128)(2,1)S(1)}, bf16[2560,256]{1,0:T(8,128)(2,1)}, u32[]{:S(2)}) %copy-start) | copy-done | bytes 1310744
  76.1 0.0 copy-start.1
  76.1 1.3 %copy-done.1 = bf16[2560,256]{1,0:T(8,128)(2,1)S(1)} copy-done((bf16[2560,256]{1,0:T(8,128)(2,1)S(1)}, bf16[2560,256]{1,0:T(8,128)(2,1)}, u32[]{:S(2)}) %copy-start.1) | copy-done | bytes 1310744
  77.4 0.0 copy-start.2
  77.4 1.1 %copy-done.2 = bf16[1280,256]{1,0:T(8,128)(2,1)S(1)} copy-done((bf16[1280,256]{1,0:T(8,128)(2,1)S(1)}, bf16[1280,256]{1,0:T(8,128)(2,1)}, u32[]{:S(2)}) %copy-start.2) | copy-done | bytes 655384
  78.5 0.0 copy-start.3
  78.5 1.1 %copy-done.3 = bf16[1280,256]{1,0:T(8,128)(2,1)S(1)} copy-done((bf16[1280,256]{1,0:T(8,128)(2,1)S(1)}, bf16[1280,256]{1,0:T(8,128)(2,1)}, u32[]{:S(2)}) %copy-start.3) | copy-done | bytes 655384
  79.6 0.0 copy-start.4
  79.6 0.8 copy-done.4
  80.5 0.0 copy-start.5
  80.5 0.8 copy-done.5
  81.3 15.3 %update.1 = (f32[2560,1280]{1,0:T(8,128)}, f32[128,128]{1,0:T(8,128)}, f32[128,128]{1,0:T(8,128)}) custom-call(f32[2560,1280]{1,0:T(8,128)} %trailing.1, bf16[2560,256]{1,0:T(8,128)(2,1)S(1)} %copy-done, bf16[2560,256]{1,0:T(8,128)(2,1)S(1)} %copy-done.1, bf16[1280,256]{1,0:T(8,128)(2,1)S(1)} %copy-done.2, bf16[1280,256]{1,0:T(8,128)(2,1)S(1)} %copy-done.3, ...), custom_call_target="tpu_custom_call" | custom-call | tf_op jit(solution)/shard_map/update/pallas_call | solution.py:470
Async XLA Ops:
  74.8 1.3 %copy-start = (bf16[2560,256]{1,0:T(8,128)(2,1)S(1)}, bf16[2560,256]{1,0:T(8,128)(2,1)}, u32[]{:S(2)}) copy-start(bf16[2560,256]{1,0:T(8,128)(2,1)} %get-tuple-element.9.left_high) | copy-start | bytes 3932164
  76.1 1.3 %copy-start.1 = (bf16[2560,256]{1,0:T(8,128)(2,1)S(1)}, bf16[2560,256]{1,0:T(8,128)(2,1)}, u32[]{:S(2)}) copy-start(bf16[2560,256]{1,0:T(8,128)(2,1)} %get-tuple-element.10.left_low) | copy-start | bytes 3932164
  77.4 1.1 %copy-start.2 = (bf16[1280,256]{1,0:T(8,128)(2,1)S(1)}, bf16[1280,256]{1,0:T(8,128)(2,1)}, u32[]{:S(2)}) copy-start(bf16[1280,256]{1,0:T(8,128)(2,1)} %get-tuple-element.11.right_high) | copy-start | bytes 1966084
  78.5 1.1 %copy-start.3 = (bf16[1280,256]{1,0:T(8,128)(2,1)S(1)}, bf16[1280,256]{1,0:T(8,128)(2,1)}, u32[]{:S(2)}) copy-start(bf16[1280,256]{1,0:T(8,128)(2,1)} %get-tuple-element.12.right_low) | copy-start | bytes 1966084
  79.6 0.8 copy-start.4
  80.5 0.8 copy-start.5

commit v3 on v2

--- a/solution.py
+++ b/solution.py
@@ -19,6 +19,9 @@
 ROW_BLOCK = SHARD * COLS
 COL_BLOCK = SHARD * ROWS
 TILE = 256
+STEP = 32
+SLOTS = 3
+WIDE = SIDE * SHARD
 
 
 def dot(first, second, contract, precision=HIGHEST):
@@ -32,13 +35,15 @@
     return high, (value - high.astype(F32)).astype(BF16)
 
 
-def factor(work, gram, step=32):
+def factor(work, gram=None, bases=range(0, NB, STEP)):
+    step = STEP
     down = lax.broadcasted_iota(jnp.int32, (NB, NB), 0)
     across = lax.broadcasted_iota(jnp.int32, (NB, NB), 1)
-    work[:, :NB] = gram
-    work[:, NB:] = jnp.where(down == across, 1.0, 0.0)
+    if gram is not None:
+        work[:, :NB] = gram
+        work[:, NB:] = jnp.where(down == across, 1.0, 0.0)
     sub = lax.broadcasted_iota(jnp.int32, (step, 1), 0)
-    for base in range(0, NB, step):
+    for base in bases:
         rows = work[base : base + step, :]
         tall = [
             jnp.broadcast_to(rows[:, base + k : base + k + 1], (step, NB)) for k in range(step)
@@ -55,8 +60,9 @@
         if base + step < NB:
             change = dot(rows[:, :NB], rows, ((0,), (0,)))
             work[base + step :, :] = work[base + step :, :] - change[base + step :, :]
-    work[:, :NB] = jnp.where(across >= down, work[:, :NB], 0.0)
-    work[:, NB:] = jnp.where(across <= down, work[:, NB:], 0.0)
+    if bases[-1] == NB - step:
+        work[:, :NB] = jnp.where(across >= down, work[:, :NB], 0.0)
+        work[:, NB:] = jnp.where(across <= down, work[:, NB:], 0.0)
 
 
 class Exchange:
@@ -127,10 +133,10 @@
 
 def panel_kernel(
     trailing_hbm, panel,
-    left_high, left_low, right_high, right_low, r_out, first_out,
-    a_full, a_high, a_low, p_rows, q_rows, q_wide, p_cols, q_cols,
+    a_full, left_high, left_low, right, r_out, first_out,
+    a_high, a_low, p_rows, q_rows, q_wide, p_cols, q_cols,
     y_part, y_mate, y_half, y_ring, y_cols, y_rows,
-    g_own, g_buf, g_part, g_all, h_own, h_buf, h_part, h_all,
+    g_own, g_buf, g_part, g_all, h_own, h_buf, h_part, h_all, s_own, s_buf, s_part, s_all,
     work_one, work_two,
     a_sem, plane_send, plane_recv, axis_send, axis_recv, ring_send, ring_recv, one_send, one_recv,
 ):
@@ -153,7 +159,6 @@
 
     load = pltpu.make_async_copy(trailing_hbm, a_full, a_sem)
     load.start()
-
     barrier = pltpu.get_barrier_semaphore()
 
     def signal(place):
@@ -196,7 +201,7 @@
         )
         gather = Exchange(
             COLS, me_c, in_plane, lambda peer: eights(full)(me_c), eights(full),
-            plane_send.at[sem + 2], plane_recv.at[sem + 2],
+            plane_send.at[sem + 3], plane_recv.at[sem + 3],
         )
 
         def total(source, count):
@@ -291,9 +296,8 @@
     receive(p_second)
 
     def basis_rows(index, carry):
-        wide = SIDE * SHARD
-        rows = pl.ds(pl.multiple_of(index * wide, wide), wide)
-        value = dot(p_rows[index].reshape(wide, NB), inverse, ((1,), (1,)))
+        rows = pl.ds(pl.multiple_of(index * WIDE, WIDE), WIDE)
+        value = dot(p_rows[index].reshape(WIDE, NB), inverse, ((1,), (1,)))
         q_rows[rows, :] = value
         high, low = split(value.T)
         q_wide[:NB, rows] = high
@@ -301,16 +305,10 @@
         return carry
 
     lax.fori_loop(0, SIDE, basis_rows, 0)
-
-    def products(index, carry):
-        cols = pl.ds(pl.multiple_of(index * TILE, TILE), TILE)
-        wide = dot(q_wide[...], a_high[:, cols], ((1,), (0,)), None)
-        value = wide[:NB, :] + wide[NB:, :]
-        value = value + dot(q_wide[:NB, :], a_low[:, cols], ((1,), (0,)), None)
-        y_part[cols, :] = value.T
-        return carry
-
-    lax.fori_loop(0, COL_BLOCK // TILE, products, 0)
+    mine = q_rows[pl.ds(pl.multiple_of(me_c * SHARD, SHARD), SHARD), :]
+    h_own[...] = dot(mine, mine, ((0,), (0,)))
+    one, two, three, more_all, more_finish = summed(h_own, h_buf, h_part, h_all, 1)
+    one()
 
     piece = lambda place, k: pl.ds(pl.multiple_of((2 * place + k) * SHARD, SHARD), SHARD)
     y_pair = [
@@ -321,8 +319,20 @@
         )
         for k in range(SIDE)
     ]
-    for item in y_pair:
-        item.start()
+
+    def products(index, carry):
+        cols = pl.ds(pl.multiple_of(index * TILE // 2, TILE // 2), TILE // 2)
+        wide = dot(q_wide[...], a_high[:, cols], ((1,), (0,)), None)
+        value = wide[:NB, :] + wide[NB:, :]
+        value = value + dot(q_wide[:NB, :], a_low[:, cols], ((1,), (0,)), None)
+        y_part[cols, :] = value.T
+        return carry
+
+    for half in range(2):
+        lax.fori_loop(5 * half, 5 * half + 5, products, 0)
+        y_pair[2 * half].start()
+        y_pair[2 * half + 1].start()
+    two()
 
     def basis_cols(index, carry):
         rows = pl.ds(pl.multiple_of(index * 2 * SHARD, 2 * SHARD), 2 * SHARD)
@@ -336,11 +346,12 @@
     y_along.start()
     p_across.receive()
     lax.fori_loop(0, SIDE, basis_cols, 0)
-    mine = q_rows[pl.ds(pl.multiple_of(me_c * SHARD, SHARD), SHARD), :]
-    h_own[:, :NB] = dot(mine, mine, ((0,), (0,)))
-    h_own[:, NB:] = dot(q_cols[...], y_part[...], ((0,), (0,)))
-    one, two, three, more_all, more_finish = summed(h_own, h_buf, h_part, h_all, 1)
-    one()
+    s_own[...] = dot(q_cols[...], y_part[...], ((0,), (0,)))
+    center_one, center_two, center_three, center_all, center_finish = summed(
+        s_own, s_buf, s_part, s_all, 2
+    )
+    center_one()
+    three()
     y_ring[z] = y_half[z]
     y_along.receive()
     y_cols[z, core] = y_ring[0] + y_ring[1] + (y_ring[2] + y_ring[3])
@@ -355,22 +366,21 @@
     ]
     y_columns, y_across = axis_gather(y_cols, 10, 8)
     start(y_swaps)
-    two()
     y_columns.start()
+    center_two()
+    more_all()
+    factor(work_two, h_all[...], range(0, NB // 2, STEP))
     receive(y_swaps)
     start(y_first)
-    three()
+    factor(work_two, None, range(NB // 2, NB, STEP))
+    center_three()
     receive(y_first)
     start(y_second)
     y_columns.receive()
     y_across.start()
-    more_all()
-
-    factor(work_two, h_all[:, :NB])
     r_out[...] = dot(work_two[:, :NB], work_one[:, :NB], ((1,), (0,)))
     second = work_two[:, NB:]
     gram_inverse = dot(second, second, ((0,), (0,)))
-    center = 4.0 * h_all[:, NB:]
 
     def finish_x(index, carry):
         rows = pl.ds(pl.multiple_of(index * TILE, TILE), TILE)
@@ -380,17 +390,23 @@
         return carry
 
     lax.fori_loop(0, ROW_BLOCK // TILE, finish_x, 0)
+    center_all()
+    center = 4.0 * s_all[...]
     y_across.receive()
 
     def finish_right(index, carry):
-        rows = pl.ds(pl.multiple_of(index * 2 * SHARD, 2 * SHARD), 2 * SHARD)
+        rows = pl.ds(pl.multiple_of(index * WIDE, WIDE), WIDE)
+        half = pl.ds(2 * index, 2)
         x_tile = dot(q_cols[rows, :], gram_inverse, ((1,), (0,)))
-        mixed = 2.0 * y_cols[index].reshape(2 * SHARD, NB) - dot(x_tile, center, ((1,), (0,)))
-        right_high[rows, :NB], right_low[rows, :NB] = split(mixed)
-        right_high[rows, NB:], right_low[rows, NB:] = split(2.0 * x_tile)
-        return carry
-
-    lax.fori_loop(0, SIDE, finish_right, 0)
+        mixed = 2.0 * y_cols[half].reshape(WIDE, NB) - dot(x_tile, center, ((1,), (0,)))
+        for place, value in ((0, mixed), (NB, 2.0 * x_tile)):
+            high, low = split(value.T)
+            right[place : place + NB, rows] = high
+            right[2 * NB + place : 3 * NB + place, rows] = low
+            right[4 * NB + place : 5 * NB + place, rows] = high
+        return carry
+
+    lax.fori_loop(0, 2, finish_right, 0)
     receive(y_second)
 
     def finish_y(index, carry):
@@ -407,6 +423,7 @@
 
     gram_finish()
     more_finish()
+    center_finish()
     for item in (*p_first, *p_second, p_swap, p_along, p_across, y_along):
         item.finish()
     for item in (*y_swaps, *y_first, *y_second, y_columns, y_across):
@@ -420,73 +437,79 @@
     f32 = lambda *dims: pltpu.VMEM(dims, F32)
     bf16 = lambda *dims: pltpu.VMEM(dims, BF16)
     dma = lambda *dims: pltpu.SemaphoreType.DMA(dims)
-    left = jax.ShapeDtypeStruct((ROW_BLOCK, 2 * NB), BF16)
-    right = jax.ShapeDtypeStruct((COL_BLOCK, 2 * NB), BF16)
-    small = jax.ShapeDtypeStruct((NB, NB), F32)
+    left, small = bf16(ROW_BLOCK, 2 * NB), f32(NB, NB)
     plane = f32(SIDE, SIDE, 2, HALF, NB)
     axis = f32(SIDE, 2, SHARD, NB)
     ring = f32(SIDE, SHARD, NB)
     return pl.pallas_call(
         panel_kernel,
-        out_shape=[left, left, right, right, small, small],
+        out_shape=[f32(ROW_BLOCK, COL_BLOCK), left, left, bf16(6 * NB, COL_BLOCK), small, small],
         in_specs=[pl.BlockSpec(memory_space=pl.ANY), vmem],
         out_specs=[vmem] * 6,
         scratch_shapes=[
-            f32(ROW_BLOCK, COL_BLOCK), bf16(ROW_BLOCK, COL_BLOCK), bf16(ROW_BLOCK, COL_BLOCK),
+            bf16(ROW_BLOCK, COL_BLOCK), bf16(ROW_BLOCK, COL_BLOCK),
             plane, f32(ROW_BLOCK, NB), bf16(2 * NB, ROW_BLOCK), axis, f32(COL_BLOCK, NB),
             f32(COL_BLOCK, NB), ring, ring, ring, axis, plane,
-            f32(NB, NB), f32(NB, NB), f32(8 * ROWS, NB), f32(NB, NB),
-            f32(NB, 2 * NB), f32(NB, 2 * NB), f32(8 * ROWS, 2 * NB), f32(NB, 2 * NB),
+            *(3 * [small, small, f32(8 * ROWS, NB), small]),
             f32(NB, 2 * NB), f32(NB, 2 * NB),
-            pltpu.SemaphoreType.DMA, dma(4, COLS), dma(4, COLS), dma(2, ROWS), dma(2, ROWS),
+            pltpu.SemaphoreType.DMA, dma(6, COLS), dma(6, COLS), dma(3, ROWS), dma(3, ROWS),
             dma(11, SIDE), dma(11, SIDE), dma(9), dma(9),
         ],
         compiler_params=pltpu.CompilerParams(
-            collective_id=0, has_side_effects=True, vmem_limit_bytes=56 * 1024 * 1024
+            collective_id=0, has_side_effects=True, vmem_limit_bytes=36 * 1024 * 1024
         ),
         name="panel",
     )(trailing, panel_block)
 
 
 def update_kernel(
-    trailing, left_high, left_low, right_high, right_low, r_in, first_in, out, r_out, first_out
+    trailing, left_high, left_low, right, r_in, first_in, out, r_out, first_out, ready, sems
 ):
-    change = dot(left_high[...], right_high[...], ((1,), (1,)), None)
-    change = change + dot(left_high[...], right_low[...], ((1,), (1,)), None)
-    change = change + dot(left_low[...], right_high[...], ((1,), (1,)), None)
-    out[...] = trailing[...] - change
-
-    @pl.when(pl.program_id(0) == 0)
-    def _():
-        r_out[...] = r_in[...]
-        first_out[...] = first_in[...]
-
-
-def update_call(trailing, left_high, left_low, right_high, right_low, r_factor, first_factor):
-    tile = pl.BlockSpec((TILE, COL_BLOCK), lambda i: (i, 0))
-    left = pl.BlockSpec((TILE, 2 * NB), lambda i: (i, 0))
-    right = pl.BlockSpec((COL_BLOCK, 2 * NB), lambda i: (0, 0))
-    small = pl.BlockSpec((NB, NB), lambda i: (0, 0))
+    def send(index, slot):
+        rows = pl.ds(pl.multiple_of(index * TILE, TILE), TILE)
+        return pltpu.make_async_copy(ready.at[slot], out.at[rows, :], sems.at[slot])
+
+    def body(index, carry):
+        slot = lax.rem(index, SLOTS)
+
+        @pl.when(index >= SLOTS)
+        def _():
+            send(index - SLOTS, slot).wait()
+
+        rows = pl.ds(pl.multiple_of(index * TILE, TILE), TILE)
+        high = left_high[rows, :]
+        left = jnp.concatenate([high, high, left_low[rows, :]], axis=1)
+        ready[slot] = trailing[rows, :] - dot(left, right[...], ((1,), (0,)), None)
+        send(index, slot).start()
+        return carry
+
+    count = ROW_BLOCK // TILE
+    lax.fori_loop(0, count, body, 0)
+    r_out[...] = r_in[...]
+    first_out[...] = first_in[...]
+    for index in range(count - SLOTS, count):
+        send(index, index % SLOTS).wait()
+
+
+def update_call(*pieces):
+    vmem = pl.BlockSpec(memory_space=pltpu.VMEM)
+    small = jax.ShapeDtypeStruct((NB, NB), F32)
     return pl.pallas_call(
         update_kernel,
-        grid=(ROW_BLOCK // TILE,),
-        out_shape=[
-            jax.ShapeDtypeStruct((ROW_BLOCK, COL_BLOCK), F32),
-            jax.ShapeDtypeStruct((NB, NB), F32),
-            jax.ShapeDtypeStruct((NB, NB), F32),
+        out_shape=[jax.ShapeDtypeStruct((ROW_BLOCK, COL_BLOCK), F32), small, small],
+        in_specs=[vmem] * 6,
+        out_specs=[pl.BlockSpec(memory_space=pltpu.HBM), vmem, vmem],
+        scratch_shapes=[
+            pltpu.VMEM((SLOTS, TILE, COL_BLOCK), F32), pltpu.SemaphoreType.DMA((SLOTS,))
         ],
-        in_specs=[tile, left, left, right, right, small, small],
-        out_specs=[tile, small, small],
-        compiler_params=pltpu.CompilerParams(
-            dimension_semantics=("arbitrary",), vmem_limit_bytes=40 * 1024 * 1024
-        ),
+        compiler_params=pltpu.CompilerParams(vmem_limit_bytes=8 * 1024 * 1024),
         name="update",
-    )(trailing, left_high, left_low, right_high, right_low, r_factor, first_factor)
+    )(*(pltpu.with_memory_space_constraint(piece, pltpu.VMEM) for piece in pieces))
 
 
 def on_device(trailing, panel_block):
     pieces = panel_call(trailing, panel_block)
-    return tuple(update_call(trailing, *pieces))
+    return tuple(update_call(*pieces))
 
 
 def solution(mesh):

time: 97.2 us -> 85.3 us (0.88)
  the two profiles are of different devices: /device:TPU:6 before, /device:TPU:1 now
where the time goes in v3:
time: 85.3 us; the launch traced here: 85.2 us
  Pallas kernels  83.5 us (98%)
  local copies, waits for them, and re-layouts  0.88 us (1%)
    pallas_call x1, Pallas kernels, panel_call(): pl.pallas_call(panel_kernel, out_shape=[f32(ROW_BLOCK, COL_BLOCK), left,...  74.9 us
    pallas_call x1, Pallas kernels, update_call(): pl.pallas_call(update_kernel, out_shape=[jax.ShapeDtypeStruct((ROW_BLOCK,...  8.64 us

profile of v3, /device:TPU:1, one launch (start us, length us, event | category | flops | bytes accessed | tf_op | source)
XLA Modules:
  0.0 85.2 jit_solution(238562490214211890)
XLA Ops:
  0.6 0.0 copy-start
  0.6 0.9 %copy-done = f32[160,128]{1,0:T(8,128)S(1)} copy-done((f32[160,128]{1,0:T(8,128)S(1)}, f32[160,128]{1,0:T(8,128)}, u32[]{:S(2)}) %copy-start) | copy-done | bytes 81944
  1.5 74.9 %panel.2 = (f32[2560,1280]{1,0:T(8,128)S(1)}, bf16[2560,256]{1,0:T(8,128)(2,1)S(1)}, bf16[2560,256]{1,0:T(8,128)(2,1)S(1)}, bf16[768,1280]{1,0:T(8,128)(2,1)S(1)...) custom-call(f32[2560,1280]{1,0:T(8,128)} %trailing_hbm.1, f32[160,128]{1,0:T(8,128)S(1)} %copy-done), custom_call_target="tpu_custom_call" | custom-call | tf_op jit(solution)/shard_map/panel/pallas_call | solution.py:444
  76.4 8.6 %update.1 = (f32[2560,1280]{1,0:T(8,128)}, f32[128,128]{1,0:T(8,128)}, f32[128,128]{1,0:T(8,128)}) custom-call(f32[2560,1280]{1,0:T(8,128)S(1)} %get-tuple-element.9.trailing, bf16[2560,256]{1,0:T(8,128)(2,1)S(1)} %get-tuple-element.10.left_high, bf16[2560,256]{1,0:T(8,128)(2,1)S(1)} %get-tuple-element.11.left_low, ...), custom_call_target="tpu_custom_call" | custom-call | tf_op jit(solution)/shard_map/update/pallas_call | solution.py:497
Async XLA Ops:
  0.6 0.9 %copy-start = (f32[160,128]{1,0:T(8,128)S(1)}, f32[160,128]{1,0:T(8,128)}, u32[]{:S(2)}) copy-start(f32[160,128]{1,0:T(8,128)} %panel.3) | copy-start | bytes 245764

commit v4 on v3

--- a/solution.py
+++ b/solution.py
@@ -33,6 +33,12 @@
 def split(value):
     high = value.astype(BF16)
     return high, (value - high.astype(F32)).astype(BF16)
+
+
+def dot3(first, second, contract):
+    (a, b), (c, d) = split(first), split(second)
+    value = dot(a, c, contract, None)
+    return value + (dot(a, d, contract, None) + dot(b, c, contract, None))
 
 
 def factor(work, gram=None, bases=range(0, NB, STEP)):
@@ -132,13 +138,13 @@
 
 
 def panel_kernel(
-    trailing_hbm, panel,
+    trailing_hbm, panel_hbm,
     a_full, left_high, left_low, right, r_out, first_out,
-    a_high, a_low, p_rows, q_rows, q_wide, p_cols, q_cols,
+    panel, x_high, x_low, mixed_t, a_high, a_low, p_rows, q_rows, q_wide, p_cols, q_cols,
     y_part, y_mate, y_half, y_ring, y_cols, y_rows,
     g_own, g_buf, g_part, g_all, h_own, h_buf, h_part, h_all, s_own, s_buf, s_part, s_all,
     work_one, work_two,
-    a_sem, plane_send, plane_recv, axis_send, axis_recv, ring_send, ring_recv, one_send, one_recv,
+    a_sem, panel_sem, plane_send, plane_recv, axis_send, axis_recv, ring_send, ring_recv, one_send, one_recv,
 ):
     me_r, me_c = lax.axis_index("row"), lax.axis_index("col")
     z, core = me_r // 2, lax.rem(me_r, 2)
@@ -157,6 +163,8 @@
     turn_c = z * SIDE + jnp.where(straight, x, SIDE - 1 - x)
     turned = jnp.logical_not(jnp.logical_and(straight, y == z))
 
+    fetch = pltpu.make_async_copy(panel_hbm, panel, panel_sem)
+    fetch.start()
     load = pltpu.make_async_copy(trailing_hbm, a_full, a_sem)
     load.start()
     barrier = pltpu.get_barrier_semaphore()
@@ -183,6 +191,7 @@
     def _():
         signal((turn_r, turn_c))
 
+    fetch.wait()
     g_own[...] = dot(panel[...], panel[...], ((0,), (0,)))
     for half in range(2):
         p_rows[y, x, half] = panel[half * HALF : (half + 1) * HALF, :]
@@ -274,9 +283,9 @@
     start(p_first)
     two()
     p_swap.start()
-    three()
     receive(p_first)
     start(p_second)
+    three()
     load.wait()
 
     def split_rows(index, carry):
@@ -291,8 +300,6 @@
     factor(work_one, g_all[...])
     first_out[...] = work_one[:, :NB]
     inverse = work_one[:, NB:]
-    p_along.receive()
-    p_across.start()
     receive(p_second)
 
     def basis_rows(index, carry):
@@ -309,6 +316,8 @@
     h_own[...] = dot(mine, mine, ((0,), (0,)))
     one, two, three, more_all, more_finish = summed(h_own, h_buf, h_part, h_all, 1)
     one()
+    p_along.receive()
+    p_across.start()
 
     piece = lambda place, k: pl.ds(pl.multiple_of((2 * place + k) * SHARD, SHARD), SHARD)
     y_pair = [
@@ -339,18 +348,18 @@
         q_cols[rows, :] = dot(p_cols[index].reshape(2 * SHARD, NB), inverse, ((1,), (1,)))
         return carry
 
+    p_across.receive()
+    lax.fori_loop(0, SIDE, basis_cols, 0)
+    s_own[...] = dot3(q_cols[...], y_part[...], ((0,), (0,)))
+    center_one, center_two, center_three, center_all, center_finish = summed(
+        s_own, s_buf, s_part, s_all, 2
+    )
+    center_one()
     for k in range(SIDE):
         y_pair[k].wait_recv()
         y_half[k] = y_part[piece(k, core), :] + y_mate[k]
     y_along = ring(in_z, z, lambda peer: y_half.at[peer], lambda slot: y_ring.at[slot], 9)
     y_along.start()
-    p_across.receive()
-    lax.fori_loop(0, SIDE, basis_cols, 0)
-    s_own[...] = dot(q_cols[...], y_part[...], ((0,), (0,)))
-    center_one, center_two, center_three, center_all, center_finish = summed(
-        s_own, s_buf, s_part, s_all, 2
-    )
-    center_one()
     three()
     y_ring[z] = y_half[z]
     y_along.receive()
@@ -369,27 +378,24 @@
     y_columns.start()
     center_two()
     more_all()
-    factor(work_two, h_all[...], range(0, NB // 2, STEP))
+    factor(work_two, h_all[...])
     receive(y_swaps)
     start(y_first)
-    factor(work_two, None, range(NB // 2, NB, STEP))
     center_three()
+    r_out[...] = dot(work_two[:, :NB], work_one[:, :NB], ((1,), (0,)))
+    second = work_two[:, NB:]
+    gram_inverse = dot(second, second, ((0,), (0,)))
+
+    def finish_x(index, carry):
+        rows = pl.ds(pl.multiple_of(index * WIDE, WIDE), WIDE)
+        x_high[rows, :], x_low[rows, :] = split(dot3(q_rows[rows, :], gram_inverse, ((1,), (0,))))
+        return carry
+
+    lax.fori_loop(0, SIDE, finish_x, 0)
     receive(y_first)
     start(y_second)
     y_columns.receive()
     y_across.start()
-    r_out[...] = dot(work_two[:, :NB], work_one[:, :NB], ((1,), (0,)))
-    second = work_two[:, NB:]
-    gram_inverse = dot(second, second, ((0,), (0,)))
-
-    def finish_x(index, carry):
-        rows = pl.ds(pl.multiple_of(index * TILE, TILE), TILE)
-        high, low = split(dot(q_rows[rows, :], gram_inverse, ((1,), (0,))))
-        left_high[rows, :NB] = high
-        left_low[rows, :NB] = low
-        return carry
-
-    lax.fori_loop(0, ROW_BLOCK // TILE, finish_x, 0)
     center_all()
     center = 4.0 * s_all[...]
     y_across.receive()
@@ -397,16 +403,25 @@
     def finish_right(index, carry):
         rows = pl.ds(pl.multiple_of(index * WIDE, WIDE), WIDE)
         half = pl.ds(2 * index, 2)
-        x_tile = dot(q_cols[rows, :], gram_inverse, ((1,), (0,)))
-        mixed = 2.0 * y_cols[half].reshape(WIDE, NB) - dot(x_tile, center, ((1,), (0,)))
-        for place, value in ((0, mixed), (NB, 2.0 * x_tile)):
+        x_tile = dot3(q_cols[rows, :], gram_inverse, ((1,), (0,)))
+        mixed = 2.0 * y_cols[half].reshape(WIDE, NB) - dot3(x_tile, center, ((1,), (0,)))
+        for target, value in ((mixed_t, mixed), (right, 2.0 * x_tile)):
             high, low = split(value.T)
-            right[place : place + NB, rows] = high
-            right[2 * NB + place : 3 * NB + place, rows] = low
-            right[4 * NB + place : 5 * NB + place, rows] = high
+            target[:NB, rows] = high
+            target[NB : 2 * NB, rows] = low
+            target[2 * NB :, rows] = high
         return carry
 
     lax.fori_loop(0, 2, finish_right, 0)
+
+    def update_x(index, carry):
+        rows = pl.ds(pl.multiple_of(index * TILE, TILE), TILE)
+        high = x_high[rows, :]
+        wide = jnp.concatenate([high, high, x_low[rows, :]], axis=1)
+        a_full[rows, :] = a_full[rows, :] - dot(wide, mixed_t[...], ((1,), (0,)), None)
+        return carry
+
+    lax.fori_loop(0, ROW_BLOCK // TILE, update_x, 0)
     receive(y_second)
 
     def finish_y(index, carry):
@@ -416,7 +431,7 @@
         source_core = jnp.where(same, core, 1 - core)
         rank = lax.rem(source_x, 2) * ROWS + 2 * down + source_core
         rows = pl.ds(pl.multiple_of(rank * SHARD, SHARD), SHARD)
-        left_high[rows, NB:], left_low[rows, NB:] = split(y_rows[down, over].reshape(SHARD, NB))
+        left_high[rows, :], left_low[rows, :] = split(y_rows[down, over].reshape(SHARD, NB))
         return carry
 
     lax.fori_loop(0, COLS, finish_y, 0)
@@ -437,29 +452,31 @@
     f32 = lambda *dims: pltpu.VMEM(dims, F32)
     bf16 = lambda *dims: pltpu.VMEM(dims, BF16)
     dma = lambda *dims: pltpu.SemaphoreType.DMA(dims)
-    left, small = bf16(ROW_BLOCK, 2 * NB), f32(NB, NB)
+    left, small = bf16(ROW_BLOCK, NB), f32(NB, NB)
+    right = bf16(3 * NB, COL_BLOCK)
     plane = f32(SIDE, SIDE, 2, HALF, NB)
     axis = f32(SIDE, 2, SHARD, NB)
     ring = f32(SIDE, SHARD, NB)
     return pl.pallas_call(
         panel_kernel,
-        out_shape=[f32(ROW_BLOCK, COL_BLOCK), left, left, bf16(6 * NB, COL_BLOCK), small, small],
-        in_specs=[pl.BlockSpec(memory_space=pl.ANY), vmem],
+        out_shape=[f32(ROW_BLOCK, COL_BLOCK), left, left, right, small, small],
+        in_specs=[pl.BlockSpec(memory_space=pl.ANY)] * 2,
         out_specs=[vmem] * 6,
         scratch_shapes=[
+            f32(SHARD, NB), left, left, right,
             bf16(ROW_BLOCK, COL_BLOCK), bf16(ROW_BLOCK, COL_BLOCK),
             plane, f32(ROW_BLOCK, NB), bf16(2 * NB, ROW_BLOCK), axis, f32(COL_BLOCK, NB),
             f32(COL_BLOCK, NB), ring, ring, ring, axis, plane,
             *(3 * [small, small, f32(8 * ROWS, NB), small]),
             f32(NB, 2 * NB), f32(NB, 2 * NB),
-            pltpu.SemaphoreType.DMA, dma(6, COLS), dma(6, COLS), dma(3, ROWS), dma(3, ROWS),
+            pltpu.SemaphoreType.DMA, pltpu.SemaphoreType.DMA, dma(6, COLS), dma(6, COLS), dma(3, ROWS), dma(3, ROWS),
             dma(11, SIDE), dma(11, SIDE), dma(9), dma(9),
         ],
         compiler_params=pltpu.CompilerParams(
             collective_id=0, has_side_effects=True, vmem_limit_bytes=36 * 1024 * 1024
         ),
         name="panel",
-    )(trailing, panel_block)
+    )(trailing, pltpu.with_memory_space_constraint(panel_block, pltpu.HBM))
 
 
 def update_kernel(

time: 85.3 us -> 83.7 us (0.981)
  local copies, waits for them, and re-layouts: 0.88 us -> 0 us
    pallas_call x1, Pallas kernels: 8.64 us -> 6.92 us  [update_call(): pl.pallas_call(update_kernel, out_shape=[jax.ShapeDtypeStruct((ROW_BLOCK,...]
    pallas_call x1, Pallas kernels: 74.9 us -> 76.1 us  [panel_call(): pl.pallas_call(panel_kernel, out_shape=[f32(ROW_BLOCK, COL_BLOCK), left,...]
    unnamed x2 -> x0, local copies, waits for them, and re-layouts: 0.88 us -> none
where the time goes in v4:
time: 83.7 us; the launch traced here: 83.6 us
  Pallas kernels  83 us (99%)
    pallas_call x1, Pallas kernels, panel_call(): pl.pallas_call(panel_kernel, out_shape=[f32(ROW_BLOCK, COL_BLOCK), left,...  76.1 us
    pallas_call x1, Pallas kernels, update_call(): pl.pallas_call(update_kernel, out_shape=[jax.ShapeDtypeStruct((ROW_BLOCK,...  6.92 us

profile of v4, /device:TPU:1, one launch (start us, length us, event | category | flops | bytes accessed | tf_op | source)
XLA Modules:
  0.0 83.6 jit_solution(7033841831581083445)
XLA Ops:
  0.6 76.1 %panel.1 = (f32[2560,1280]{1,0:T(8,128)S(1)}, bf16[2560,128]{1,0:T(8,128)(2,1)S(1)}, bf16[2560,128]{1,0:T(8,128)(2,1)S(1)}, bf16[384,1280]{1,0:T(8,128)(2,1)S(1)...) custom-call(f32[2560,1280]{1,0:T(8,128)} %trailing_hbm.1, f32[160,128]{1,0:T(8,128)} %panel_hbm.1), custom_call_target="tpu_custom_call" | custom-call | tf_op jit(solution)/shard_map/panel/pallas_call | solution.py:460
  76.7 6.9 %update.1 = (f32[2560,1280]{1,0:T(8,128)}, f32[128,128]{1,0:T(8,128)}, f32[128,128]{1,0:T(8,128)}) custom-call(f32[2560,1280]{1,0:T(8,128)S(1)} %get-tuple-element.9.trailing, bf16[2560,128]{1,0:T(8,128)(2,1)S(1)} %get-tuple-element.10.left_high, bf16[2560,128]{1,0:T(8,128)(2,1)S(1)} %get-tuple-element.11.left_low, ...), custom_call_target="tpu_custom_call" | custom-call | tf_op jit(solution)/shard_map/update/pallas_call | solution.py:514

commit v5 on v4

--- a/solution.py
+++ b/solution.py
@@ -77,12 +77,16 @@
         self.source, self.target = source, target
         self.send_sem, self.recv_sem = send_sem, recv_sem
 
-    def each(self, action):
+    def each(self, action, unroll=False):
         def body(step, carry):
             action(lax.rem(self.me + step, self.size))
             return carry
 
-        lax.fori_loop(1, self.size, body, 0)
+        if unroll or self.size == SIDE:
+            for step in range(1, self.size):
+                body(step, 0)
+        else:
+            lax.fori_loop(1, self.size, body, 0)
 
     def copy(self, peer, slot):
         return pltpu.make_async_remote_copy(
@@ -95,7 +99,7 @@
         )
 
     def start(self):
-        self.each(lambda peer: self.copy(peer, self.me).start())
+        self.each(lambda peer: self.copy(peer, self.me).start(), unroll=True)
 
     def receive(self):
         self.each(lambda peer: self.copy(peer, peer).wait_recv())
@@ -330,15 +334,15 @@
     ]
 
     def products(index, carry):
-        cols = pl.ds(pl.multiple_of(index * TILE // 2, TILE // 2), TILE // 2)
+        cols = pl.ds(pl.multiple_of(index * TILE, TILE), TILE)
         wide = dot(q_wide[...], a_high[:, cols], ((1,), (0,)), None)
         value = wide[:NB, :] + wide[NB:, :]
         value = value + dot(q_wide[:NB, :], a_low[:, cols], ((1,), (0,)), None)
         y_part[cols, :] = value.T
         return carry
 
-    for half in range(2):
-        lax.fori_loop(5 * half, 5 * half + 5, products, 0)
+    for half, (begin, end) in enumerate(((0, 3), (3, 5))):
+        lax.fori_loop(begin, end, products, 0)
         y_pair[2 * half].start()
         y_pair[2 * half + 1].start()
     two()
@@ -362,6 +366,9 @@
     y_along.start()
     three()
     y_ring[z] = y_half[z]
+    gram_finish()
+    for item in (*p_first, *p_second, p_swap, p_along):
+        item.finish()
     y_along.receive()
     y_cols[z, core] = y_ring[0] + y_ring[1] + (y_ring[2] + y_ring[3])
     y_first, y_second = plane_gather(y_rows, 4)
@@ -422,6 +429,12 @@
         return carry
 
     lax.fori_loop(0, ROW_BLOCK // TILE, update_x, 0)
+    more_finish()
+    center_finish()
+    for item in (p_across, y_along, *y_swaps, *y_first, y_columns):
+        item.finish()
+    for item in y_pair:
+        item.wait_send()
     receive(y_second)
 
     def finish_y(index, carry):
@@ -436,15 +449,8 @@
 
     lax.fori_loop(0, COLS, finish_y, 0)
 
-    gram_finish()
-    more_finish()
-    center_finish()
-    for item in (*p_first, *p_second, p_swap, p_along, p_across, y_along):
+    for item in (*y_second, y_across):
         item.finish()
-    for item in (*y_swaps, *y_first, *y_second, y_columns, y_across):
-        item.finish()
-    for item in y_pair:
-        item.wait_send()
 
 
 def panel_call(trailing, panel_block):

time: 83.7 us -> 79.8 us (0.953)
  Pallas kernels: 83 us -> 78.9 us
    pallas_call x1, Pallas kernels: 76.1 us -> 72 us  [panel_call(): pl.pallas_call(panel_kernel, out_shape=[f32(ROW_BLOCK, COL_BLOCK), left,...]
where the time goes in v5:
time: 79.8 us; the launch traced here: 79.7 us
  Pallas kernels  78.9 us (99%)
  between operations  0.8 us (1%)
    pallas_call x1, Pallas kernels, panel_call(): pl.pallas_call(panel_kernel, out_shape=[f32(ROW_BLOCK, COL_BLOCK), left,...  72 us
    pallas_call x1, Pallas kernels, update_call(): pl.pallas_call(update_kernel, out_shape=[jax.ShapeDtypeStruct((ROW_BLOCK,...  6.92 us

profile of v5, /device:TPU:1, one launch (start us, length us, event | category | flops | bytes accessed | tf_op | source)
XLA Modules:
  0.0 79.7 jit_solution(1179493768455474605)
XLA Ops:
  0.6 72.0 %panel.1 = (f32[2560,1280]{1,0:T(8,128)S(1)}, bf16[2560,128]{1,0:T(8,128)(2,1)S(1)}, bf16[2560,128]{1,0:T(8,128)(2,1)S(1)}, bf16[384,1280]{1,0:T(8,128)(2,1)S(1)...) custom-call(f32[2560,1280]{1,0:T(8,128)} %trailing_hbm.1, f32[160,128]{1,0:T(8,128)} %panel_hbm.1), custom_call_target="tpu_custom_call" | custom-call | tf_op jit(solution)/shard_map/panel/pallas_call | solution.py:466
  72.6 6.9 %update.1 = (f32[2560,1280]{1,0:T(8,128)}, f32[128,128]{1,0:T(8,128)}, f32[128,128]{1,0:T(8,128)}) custom-call(f32[2560,1280]{1,0:T(8,128)S(1)} %get-tuple-element.9.trailing, bf16[2560,128]{1,0:T(8,128)(2,1)S(1)} %get-tuple-element.10.left_high, bf16[2560,128]{1,0:T(8,128)(2,1)S(1)} %get-tuple-element.11.left_low, ...), custom_call_target="tpu_custom_call" | custom-call | tf_op jit(solution)/shard_map/update/pallas_call | solution.py:520

commit v6 on v5

--- a/solution.py
+++ b/solution.py
@@ -102,7 +102,7 @@
         self.each(lambda peer: self.copy(peer, self.me).start(), unroll=True)
 
     def receive(self):
-        self.each(lambda peer: self.copy(peer, peer).wait_recv())
+        self.each(lambda peer: self.copy(peer, peer).wait_recv(), unroll=True)
 
     def finish(self):
         self.each(lambda peer: self.copy(peer, peer).wait_send())
@@ -177,11 +177,8 @@
         pl.semaphore_signal(barrier, inc=1, device_id=place, device_id_type=MESH)
 
     def greet(size, me, place):
-        def body(step, carry):
+        for step in range(1, size):
             signal(place(lax.rem(me + step, size)))
-            return carry
-
-        lax.fori_loop(1, size, body, 0)
 
     greet(COLS, me_c, in_plane)
     greet(ROWS, me_r, in_axis)
@@ -283,8 +280,8 @@
         out_r, me_r, one_send.at[0], one_recv.at[0],
     )
     p_along, p_across = axis_gather(p_cols, 8, 1)
+    start(p_first)
     one()
-    start(p_first)
     two()
     p_swap.start()
     receive(p_first)
@@ -365,6 +362,7 @@
     y_along = ring(in_z, z, lambda peer: y_half.at[peer], lambda slot: y_ring.at[slot], 9)
     y_along.start()
     three()
+    center_two()
     y_ring[z] = y_half[z]
     gram_finish()
     for item in (*p_first, *p_second, p_swap, p_along):
@@ -383,13 +381,11 @@
     y_columns, y_across = axis_gather(y_cols, 10, 8)
     start(y_swaps)
     y_columns.start()
-    center_two()
     more_all()
     factor(work_two, h_all[...])
+    center_three()
     receive(y_swaps)
     start(y_first)
-    center_three()
-    r_out[...] = dot(work_two[:, :NB], work_one[:, :NB], ((1,), (0,)))
     second = work_two[:, NB:]
     gram_inverse = dot(second, second, ((0,), (0,)))
 
@@ -422,13 +418,14 @@
     lax.fori_loop(0, 2, finish_right, 0)
 
     def update_x(index, carry):
-        rows = pl.ds(pl.multiple_of(index * TILE, TILE), TILE)
+        rows = pl.ds(pl.multiple_of(index * 2 * TILE, 2 * TILE), 2 * TILE)
         high = x_high[rows, :]
         wide = jnp.concatenate([high, high, x_low[rows, :]], axis=1)
         a_full[rows, :] = a_full[rows, :] - dot(wide, mixed_t[...], ((1,), (0,)), None)
         return carry
 
-    lax.fori_loop(0, ROW_BLOCK // TILE, update_x, 0)
+    lax.fori_loop(0, ROW_BLOCK // (2 * TILE), update_x, 0)
+    r_out[...] = dot(work_two[:, :NB], work_one[:, :NB], ((1,), (0,)))
     more_finish()
     center_finish()
     for item in (p_across, y_along, *y_swaps, *y_first, y_columns):

time: 79.8 us -> 79.9 us (level)
  no operation moved by 1% of the time
where the time goes in v6:
time: 79.9 us; the launch traced here: 79.8 us
  Pallas kernels  79 us (99%)
  between operations  0.8 us (1%)
    pallas_call x1, Pallas kernels, panel_call(): pl.pallas_call(panel_kernel, out_shape=[f32(ROW_BLOCK, COL_BLOCK), left,...  72.1 us
    pallas_call x1, Pallas kernels, update_call(): pl.pallas_call(update_kernel, out_shape=[jax.ShapeDtypeStruct((ROW_BLOCK,...  6.92 us

profile of v6, /device:TPU:1, one launch (start us, length us, event | category | flops | bytes accessed | tf_op | source)
XLA Modules:
  0.0 79.8 jit_solution(8642421914253250759)
XLA Ops:
  0.6 72.1 %panel.1 = (f32[2560,1280]{1,0:T(8,128)S(1)}, bf16[2560,128]{1,0:T(8,128)(2,1)S(1)}, bf16[2560,128]{1,0:T(8,128)(2,1)S(1)}, bf16[384,1280]{1,0:T(8,128)(2,1)S(1)...) custom-call(f32[2560,1280]{1,0:T(8,128)} %trailing_hbm.1, f32[160,128]{1,0:T(8,128)} %panel_hbm.1), custom_call_target="tpu_custom_call" | custom-call | tf_op jit(solution)/shard_map/panel/pallas_call | solution.py:463
  72.7 6.9 %update.1 = (f32[2560,1280]{1,0:T(8,128)}, f32[128,128]{1,0:T(8,128)}, f32[128,128]{1,0:T(8,128)}) custom-call(f32[2560,1280]{1,0:T(8,128)S(1)} %get-tuple-element.9.trailing, bf16[2560,128]{1,0:T(8,128)(2,1)S(1)} %get-tuple-element.10.left_high, bf16[2560,128]{1,0:T(8,128)(2,1)S(1)} %get-tuple-element.11.left_low, ...), custom_call_target="tpu_custom_call" | custom-call | tf_op jit(solution)/shard_map/update/pallas_call | solution.py:517

commit v7 on v6

--- a/solution.py
+++ b/solution.py
@@ -163,8 +163,8 @@
     in_r, in_c = me_c // 2, ROWS * lax.rem(me_c, 2) + me_r
     apart = jnp.logical_not(jnp.logical_and(out_r == me_r, out_c == me_c))
     straight = core == x // 2
-    turn_r = 2 * y + jnp.where(straight, core, 1 - core)
-    turn_c = z * SIDE + jnp.where(straight, x, SIDE - 1 - x)
+    turn_r = 2 * y + x // 2
+    turn_x = jnp.where(straight, x, SIDE - 1 - x)
     turned = jnp.logical_not(jnp.logical_and(straight, y == z))
 
     fetch = pltpu.make_async_copy(panel_hbm, panel, panel_sem)
@@ -188,16 +188,23 @@
         signal((out_r, out_c))
         signal((in_r, in_c))
 
-    @pl.when(turned)
-    def _():
-        signal((turn_r, turn_c))
+    away = lambda half, j: jnp.logical_or(turned, j != (y, x)[half])
+    for j in range(SIDE):
+
+        @pl.when(away(0, j))
+        def _():
+            signal((2 * j + x // 2, z * SIDE + turn_x))
+
+        @pl.when(away(1, j))
+        def _():
+            signal((2 * y + j // 2, z * SIDE + jnp.where(core == j // 2, j, SIDE - 1 - j)))
 
     fetch.wait()
     g_own[...] = dot(panel[...], panel[...], ((0,), (0,)))
     for half in range(2):
         p_rows[y, x, half] = panel[half * HALF : (half + 1) * HALF, :]
     pl.semaphore_wait(
-        barrier, COLS + ROWS - 2 + jnp.where(apart, 2, 0) + jnp.where(turned, 1, 0)
+        barrier, COLS + ROWS - 2 + jnp.where(apart, 2, 0) + jnp.where(turned, 8, 6)
     )
 
     def summed(own, buf, part, full, sem):
@@ -369,23 +376,38 @@
         item.finish()
     y_along.receive()
     y_cols[z, core] = y_ring[0] + y_ring[1] + (y_ring[2] + y_ring[3])
-    y_first, y_second = plane_gather(y_rows, 4)
-    y_swaps = [
-        Swap(
-            turned, (turn_r, turn_c), y_cols.at[z, core, pl.ds(half * HALF, HALF)],
-            lambda slot, half=half: y_rows.at[slot // SIDE, lax.rem(slot, SIDE), half],
-            turn_c, me_c, one_send.at[2 + half], one_recv.at[2 + half],
-        )
-        for half in range(2)
-    ]
+    _, y_second = plane_gather(y_rows, 4)
+
+    def y_copy(half, j, slot, recv):
+        place = (turn_r, j * SIDE + turn_x) if half == 0 else (turn_r, z * SIDE + j)
+        return pltpu.make_async_remote_copy(
+            src_ref=y_cols.at[z, core, pl.ds(half * HALF, HALF)],
+            dst_ref=y_rows.at[slot[0], slot[1], half],
+            send_sem=ring_send.at[4 + half, j], recv_sem=ring_recv.at[4 + half, recv],
+            device_id=place, device_id_type=MESH,
+        )
+
+    def y_each(action):
+        for j in range(SIDE):
+            for half in range(2):
+
+                @pl.when(away(half, j))
+                def _(half=half, j=j):
+                    action(half, j)
+
+    there = (z, turn_x)
+    y_each(lambda half, j: y_copy(half, j, there, there[half]).start())
+
+    @pl.when(jnp.logical_not(turned))
+    def _():
+        for half in range(2):
+            y_rows[y, x, half] = y_cols[z, core, pl.ds(half * HALF, HALF)]
+
     y_columns, y_across = axis_gather(y_cols, 10, 8)
-    start(y_swaps)
     y_columns.start()
     more_all()
     factor(work_two, h_all[...])
     center_three()
-    receive(y_swaps)
-    start(y_first)
     second = work_two[:, NB:]
     gram_inverse = dot(second, second, ((0,), (0,)))
 
@@ -395,7 +417,7 @@
         return carry
 
     lax.fori_loop(0, SIDE, finish_x, 0)
-    receive(y_first)
+    y_each(lambda half, j: y_copy(half, j, (j, x) if half == 0 else (y, j), j).wait_recv())
     start(y_second)
     y_columns.receive()
     y_across.start()
@@ -428,10 +450,11 @@
     r_out[...] = dot(work_two[:, :NB], work_one[:, :NB], ((1,), (0,)))
     more_finish()
     center_finish()
-    for item in (p_across, y_along, *y_swaps, *y_first, y_columns):
+    for item in (p_across, y_along, y_columns):
         item.finish()
     for item in y_pair:
         item.wait_send()
+    y_each(lambda half, j: y_copy(half, j, there, there[half]).wait_send())
     receive(y_second)
 
     def finish_y(index, carry):

time: 79.9 us -> 82.7 us (1.035)
  Pallas kernels: 79 us -> 81.8 us
    pallas_call x1, Pallas kernels: 72.1 us -> 74.9 us  [panel_call(): pl.pallas_call(panel_kernel, out_shape=[f32(ROW_BLOCK, COL_BLOCK), left,...]
where the time goes in v7:
time: 82.7 us; the launch traced here: 82.6 us
  Pallas kernels  81.8 us (99%)
    pallas_call x1, Pallas kernels, panel_call(): pl.pallas_call(panel_kernel, out_shape=[f32(ROW_BLOCK, COL_BLOCK), left,...  74.9 us
    pallas_call x1, Pallas kernels, update_call(): pl.pallas_call(update_kernel, out_shape=[jax.ShapeDtypeStruct((ROW_BLOCK,...  6.92 us

profile of v7, /device:TPU:1, one launch (start us, length us, event | category | flops | bytes accessed | tf_op | source)
XLA Modules:
  0.0 82.6 jit_solution(1136730451439674984)
XLA Ops:
  0.6 74.9 %panel.1 = (f32[2560,1280]{1,0:T(8,128)S(1)}, bf16[2560,128]{1,0:T(8,128)(2,1)S(1)}, bf16[2560,128]{1,0:T(8,128)(2,1)S(1)}, bf16[384,1280]{1,0:T(8,128)(2,1)S(1)...) custom-call(f32[2560,1280]{1,0:T(8,128)} %trailing_hbm.1, f32[160,128]{1,0:T(8,128)} %panel_hbm.1), custom_call_target="tpu_custom_call" | custom-call | tf_op jit(solution)/shard_map/panel/pallas_call | solution.py:486
  75.5 6.9 %update.1 = (f32[2560,1280]{1,0:T(8,128)}, f32[128,128]{1,0:T(8,128)}, f32[128,128]{1,0:T(8,128)}) custom-call(f32[2560,1280]{1,0:T(8,128)S(1)} %get-tuple-element.9.trailing, bf16[2560,128]{1,0:T(8,128)(2,1)S(1)} %get-tuple-element.10.left_high, bf16[2560,128]{1,0:T(8,128)(2,1)S(1)} %get-tuple-element.11.left_low, ...), custom_call_target="tpu_custom_call" | custom-call | tf_op jit(solution)/shard_map/update/pallas_call | solution.py:540

commit v8 on v5

--- a/solution.py
+++ b/solution.py
@@ -20,7 +20,8 @@
 COL_BLOCK = SHARD * ROWS
 TILE = 256
 STEP = 32
-SLOTS = 3
+SLOTS = 2
+LAST = 512
 WIDE = SIDE * SHARD
 
 
@@ -489,7 +490,7 @@
     trailing, left_high, left_low, right, r_in, first_in, out, r_out, first_out, ready, sems
 ):
     def send(index, slot):
-        rows = pl.ds(pl.multiple_of(index * TILE, TILE), TILE)
+        rows = pl.ds(pl.multiple_of(index * LAST, LAST), LAST)
         return pltpu.make_async_copy(ready.at[slot], out.at[rows, :], sems.at[slot])
 
     def body(index, carry):
@@ -499,14 +500,14 @@
         def _():
             send(index - SLOTS, slot).wait()
 
-        rows = pl.ds(pl.multiple_of(index * TILE, TILE), TILE)
+        rows = pl.ds(pl.multiple_of(index * LAST, LAST), LAST)
         high = left_high[rows, :]
         left = jnp.concatenate([high, high, left_low[rows, :]], axis=1)
         ready[slot] = trailing[rows, :] - dot(left, right[...], ((1,), (0,)), None)
         send(index, slot).start()
         return carry
 
-    count = ROW_BLOCK // TILE
+    count = ROW_BLOCK // LAST
     lax.fori_loop(0, count, body, 0)
     r_out[...] = r_in[...]
     first_out[...] = first_in[...]
@@ -523,9 +524,9 @@
         in_specs=[vmem] * 6,
         out_specs=[pl.BlockSpec(memory_space=pltpu.HBM), vmem, vmem],
         scratch_shapes=[
-            pltpu.VMEM((SLOTS, TILE, COL_BLOCK), F32), pltpu.SemaphoreType.DMA((SLOTS,))
+            pltpu.VMEM((SLOTS, LAST, COL_BLOCK), F32), pltpu.SemaphoreType.DMA((SLOTS,))
         ],
-        compiler_params=pltpu.CompilerParams(vmem_limit_bytes=8 * 1024 * 1024),
+        compiler_params=pltpu.CompilerParams(vmem_limit_bytes=12 * 1024 * 1024),
         name="update",
     )(*(pltpu.with_memory_space_constraint(piece, pltpu.VMEM) for piece in pieces))
 

time: 79.8 us -> 80.6 us (1.010)
  no operation moved by 1% of the time
where the time goes in v8:
time: 80.6 us; the launch traced here: 80.5 us
  Pallas kernels  79.7 us (99%)
    pallas_call x1, Pallas kernels, panel_call(): pl.pallas_call(panel_kernel, out_shape=[f32(ROW_BLOCK, COL_BLOCK), left,...  72 us
    pallas_call x1, Pallas kernels, update_call(): pl.pallas_call(update_kernel, out_shape=[jax.ShapeDtypeStruct((ROW_BLOCK,...  7.67 us

profile of v8, /device:TPU:1, one launch (start us, length us, event | category | flops | bytes accessed | tf_op | source)
XLA Modules:
  0.0 80.5 jit_solution(1020042363719515889)
XLA Ops:
  0.6 72.0 %panel.1 = (f32[2560,1280]{1,0:T(8,128)S(1)}, bf16[2560,128]{1,0:T(8,128)(2,1)S(1)}, bf16[2560,128]{1,0:T(8,128)(2,1)S(1)}, bf16[384,1280]{1,0:T(8,128)(2,1)S(1)...) custom-call(f32[2560,1280]{1,0:T(8,128)} %trailing_hbm.1, f32[160,128]{1,0:T(8,128)} %panel_hbm.1), custom_call_target="tpu_custom_call" | custom-call | tf_op jit(solution)/shard_map/panel/pallas_call | solution.py:467
  72.6 7.7 %update.1 = (f32[2560,1280]{1,0:T(8,128)}, f32[128,128]{1,0:T(8,128)}, f32[128,128]{1,0:T(8,128)}) custom-call(f32[2560,1280]{1,0:T(8,128)S(1)} %get-tuple-element.9.trailing, bf16[2560,128]{1,0:T(8,128)(2,1)S(1)} %get-tuple-element.10.left_high, bf16[2560,128]{1,0:T(8,128)(2,1)S(1)} %get-tuple-element.11.left_low, ...), custom_call_target="tpu_custom_call" | custom-call | tf_op jit(solution)/shard_map/update/pallas_call | solution.py:521
